TPU v7x, 256 devices: a whole 4x4x8 slice. The times are simulated.
256 devices in a mesh: band: 128 (over y, x, z), lev: 2 (over core).
Axes of the slice: x: 4, y: 4, z: 8, core: 2. Of those that a mesh axis runs over, the one named last changes fastest.
Arguments:
- fourier_in: bfloat16 [1280, 2, 8, 4, 1280], P('band', None, 'lev'), may hold values from -6 to 6
- row_points: int32 [1280], P('band'), may hold values from 20 to 5144, as said below
- gauss_weight: float32 [1280], P('band'), may hold values from 0.5 to 1.5
- pair_order: int32 [640], replicated, may hold values from 0 to 639, each once
- legendre: bfloat16 [640, 1281, 1280], P('band', None, 'lev'), may hold values from -0.25 to 0.25
- diffusion: float32 [8, 2], replicated, may hold values from 0.1 to 10
Outputs:
- fourier_out: bfloat16 [1280, 2, 8, 4, 1280], P('band', None, 'lev')
Inputs may be any that keep to these rules, and one draw needn't show every extreme that they name: `row_points`: row i holds 20 + 4 i, 24 + 4 i or 28 + 4 i points; the last row holds 28 + 4 (1279). `pair_order`: every pair index appears once.
All inputs are finite; a program needn't handle non-finite values.
Results may differ from a plain program's by a relative error of at most 0.0063.
Values may be sent and summed in bfloat16 or wider, within the bound.
No kernel may reach another device: no remote copies, remote signals or barrier semaphores. Data moves between devices by JAX's collectives and lax.ppermute only.
A program may use at most 128 MiB of HBM per device.

v0:
```python
import jax
import jax.numpy as jnp
from jax import lax
from jax.sharding import PartitionSpec as P


def make_live(row_points, orders):
    cutoff = jnp.minimum(orders - 1, (row_points - 1) // 2)
    column = lax.broadcasted_iota(jnp.int32, (row_points.shape[0], orders), 1)
    return (column <= cutoff[:, None]).astype(jnp.float32)


def row_layout(first_order, orders):
    midpoint = orders // 2
    row_index = jnp.arange(orders + 1, dtype=jnp.int32)
    odd_block = (row_index > midpoint).astype(jnp.int32)
    position = row_index - odd_block * (midpoint + 1)
    boundary = jnp.where(
        odd_block[None, :] == 1,
        ((orders - first_order) // 2)[:, None],
        ((orders + 1 - first_order) // 2)[:, None],
    )
    leading = position[None, :] < boundary
    second_order = orders - 1 - first_order
    degree = jnp.where(
        leading,
        first_order[:, None] + odd_block[None, :] + 2 * position[None, :],
        second_order[:, None] + odd_block[None, :] + 2 * (position[None, :] - boundary),
    )
    return (leading, degree)


def damping(kappa_rows, degree, orders):
    kappas = jnp.repeat(kappa_rows, 2, axis=1)
    growth = (degree * (degree + 1)).astype(jnp.float32) / float(orders * (orders + 1))
    return 1.0 / (1.0 + kappas[:, :, None, None] * growth[None, None])


def legendre_forward(arrived, tables, leading, midpoint):
    slots = tables.shape[0]
    nrows = tables.shape[1]
    levels = arrived.shape[2]
    grouped = arrived.reshape(2, arrived.shape[1], levels, 4, slots, 2)
    product = jnp.einsum("srl,plvcsq->sqpvcr", tables, grouped, preferred_element_type=jnp.float32)
    odd_rows = (jnp.arange(nrows, dtype=jnp.int32) > midpoint)[None, None, None, :]
    lead_rows = leading[:, None, None, :]
    picked = jnp.where(
        lead_rows,
        jnp.where(odd_rows, product[:, 0, 1], product[:, 0, 0]),
        jnp.where(odd_rows, product[:, 1, 1], product[:, 1, 0]),
    )
    return jnp.transpose(picked, (1, 2, 0, 3))


def legendre_inverse(spectral, tables, leading, midpoint):
    slots = tables.shape[0]
    nrows = tables.shape[1]
    levels = spectral.shape[0]
    by_slot = jnp.transpose(spectral, (2, 0, 1, 3))
    odd_rows = (jnp.arange(nrows, dtype=jnp.int32) > midpoint)[None, None, None, :]
    lead_rows = leading[:, None, None, :]
    zeroes = jnp.zeros_like(by_slot)
    chosen = jnp.stack(
        [
            jnp.stack(
                [
                    jnp.where(lead_rows & ~odd_rows, by_slot, zeroes),
                    jnp.where(lead_rows & odd_rows, by_slot, zeroes),
                ],
                axis=1,
            ),
            jnp.stack(
                [
                    jnp.where(~lead_rows & ~odd_rows, by_slot, zeroes),
                    jnp.where(~lead_rows & odd_rows, by_slot, zeroes),
                ],
                axis=1,
            ),
        ],
        axis=1,
    )
    summed = jnp.einsum(
        "srl,sqpvcr->plvcsq", tables, chosen, preferred_element_type=jnp.float32
    ).astype(jnp.bfloat16)
    return summed.reshape(2, tables.shape[2], levels, 4, 2 * slots)


def on_device(fourier_in, row_points, gauss_weight, pair_order, legendre, diffusion):
    orders = fourier_in.shape[-1]
    midpoint = orders // 2
    slot_count = legendre.shape[0]
    live_cells = make_live(row_points, orders)
    factor = (live_cells * gauss_weight[:, None])[:, None, None, :]
    widened = fourier_in.astype(jnp.float32)
    even_part = ((widened[:, 0] + widened[:, 1]) * factor).astype(jnp.bfloat16)
    odd_part = ((widened[:, 0] - widened[:, 1]) * factor).astype(jnp.bfloat16)
    listing = jnp.stack([pair_order, orders - 1 - pair_order], axis=1).reshape(-1)
    column = lax.broadcasted_iota(jnp.int32, (orders, orders), 1)
    selector = (listing[:, None] == column).astype(jnp.bfloat16)
    outgoing = jnp.einsum(
        "pivcm,km->pivck",
        jnp.stack([even_part, odd_part]),
        selector,
        preferred_element_type=jnp.float32,
    ).astype(jnp.bfloat16)
    my_pairs = lax.dynamic_slice_in_dim(
        pair_order, lax.axis_index("band") * slot_count, slot_count, 0
    )
    leading, degree = row_layout(my_pairs, orders)
    arrived = lax.all_to_all(
        lax.all_to_all(outgoing, "band", split_axis=4, concat_axis=1, tiled=True),
        "lev",
        split_axis=1,
        concat_axis=2,
        tiled=True,
    )
    coeffs = lax.psum(legendre_forward(arrived, legendre, leading, midpoint), "lev")
    spectral = (coeffs * damping(diffusion, degree, orders)).astype(jnp.bfloat16)
    produced = legendre_inverse(spectral, legendre, leading, midpoint)
    returning = lax.all_to_all(produced, "lev", split_axis=2, concat_axis=1, tiled=True)
    landed = lax.all_to_all(returning, "band", split_axis=1, concat_axis=4, tiled=True)
    placed = jnp.einsum("pivck,km->pivcm", landed, selector, preferred_element_type=jnp.float32)
    cell_mask = live_cells[:, None, None, :]
    fourier_out = jnp.stack(
        [(placed[0] + placed[1]) * cell_mask, (placed[0] - placed[1]) * cell_mask], axis=1
    )
    return fourier_out.astype(jnp.bfloat16)


def solution(mesh):
    in_specs = (
        P("band", None, "lev", None, None),
        P("band"),
        P("band"),
        P(),
        P("band", None, "lev"),
        P(),
    )
    out_specs = P("band", None, "lev", None, None)
    return jax.shard_map(
        on_device, mesh=mesh, in_specs=in_specs, out_specs=out_specs, check_vma=False
    )
```

profile of v0, /device:TPU:1, one launch (start us, length us, event | category | flops | bytes accessed | tf_op | source)
XLA Modules:
  0.0 427.3 jit_solution(3689476104091468286)
XLA Ops:
  10.5 2.1 fusion.14
  12.6 10.7 %copy.63 = bf16[2,10,4,4,1280]{1,3,2,0,4:T(4,128)(2,1)} copy(bf16[2,10,4,4,1280]{4,1,3,2,0:T(8,128)(2,1)S(1)} %fusion.14) | data formatting | bytes 1638400 | tf_op jit(solution)/shard_map/convert_element_type | solution.py:105
  23.3 18.5 %reshape.565 = bf16[128,2,1600]{2,1,0:T(2,128)(2,1)} reshape(bf16[1280,2,4,4,10]{4,3,2,1,0:T(4,128)(2,1)} %bitcast.118) | data formatting | bytes 1638400
  41.8 16.3 %all-to-all-start = ((bf16[128,2,1600]{2,1,0:T(2,128)(2,1)}), bf16[128,2,1600]{2,1,0:T(2,128)(2,1)S(1)}, u32[]{:S(2)}, u32[]{:S(2)}) async-start(bf16[128,2,1600]{2,1,0:T(2,128)(2,1)} %reshape.565), calls=%async_computation | async-start | bytes 1703936 | tf_op jit(solution)/shard_map/all_to_all | solution.py:111
  59.1 25.0 %all-to-all-done = bf16[128,2,1600]{2,1,0:T(2,128)(2,1)S(1)} async-done(((bf16[128,2,1600]{2,1,0:T(2,128)(2,1)}), bf16[128,2,1600]{2,1,0:T(2,128)(2,1)S(1)}, u32[]{:S(2)}, u32[]{:S(2)}) %all-to-all-start) | async-done | bytes 819232 | tf_op jit(solution)/shard_map/all_to_all | solution.py:111
  84.1 25.9 %reshape.566 = bf16[1280,2,4,4,10]{4,3,2,1,0:T(4,128)(2,1)} reshape(bf16[128,2,1600]{2,1,0:T(2,128)(2,1)S(1)} %all-to-all-done) | data formatting | bytes 1638400
  110.0 20.3 %copy.106 = bf16[2,10,4,4,128,10]{1,4,3,5,2,0:T(8,128)(2,1)} copy(bf16[2,10,4,4,128,10]{1,3,2,0,5,4:T(4,128)(2,1)} %bitcast.119) | data formatting | bytes 1638400 | tf_op jit(solution)/shard_map/all_to_all | solution.py:111
  130.3 32.6 %copy.85 = bf16[2,128,10,4,4,10]{5,4,3,0,2,1:T(4,128)(2,1)} copy(bf16[2,128,10,4,4,10]{2,1,4,5,3,0:T(8,128)(2,1)} %bitcast.120) | data formatting | bytes 1638400 | tf_op jit(solution)/shard_map/all_to_all | solution.py:111
  162.9 27.9 %reshape.567 = bf16[2,2,102400]{2,1,0:T(2,128)(2,1)S(1)} reshape(bf16[1280,2,4,4,10]{4,3,2,1,0:T(4,128)(2,1)} %bitcast.121) | data formatting | bytes 1638400
  190.8 7.1 %all_to_all.69 = bf16[2,2,102400]{2,1,0:T(2,128)(2,1)S(1)} all-to-all(bf16[2,2,102400]{2,1,0:T(2,128)(2,1)S(1)} %reshape.567), channel_id=1, replica_groups=mesh['band'=128,'lev'=2] {'lev'}, dimensions={0} | all-to-all | bytes 1638400 | tf_op jit(solution)/shard_map/all_to_all | solution.py:110
  197.9 30.2 %reshape.568 = bf16[1280,2,4,4,10]{4,3,2,1,0:T(4,128)(2,1)} reshape(bf16[2,2,102400]{2,1,0:T(2,128)(2,1)S(1)} %all_to_all.69) | data formatting | bytes 1638400
  228.0 13.3 %copy.67 = bf16[2,2,640,4,4,10]{2,4,5,3,1,0:T(4,128)(2,1)S(1)} copy(bf16[2,2,640,4,4,10]{5,4,3,0,2,1:T(4,128)(2,1)} %bitcast.122) | data formatting | bytes 1638400 | tf_op jit(solution)/shard_map/all_to_all | solution.py:110
  241.3 6.1 %fusion.9 = f32[5,2,2,8,4,1281]{5,3,1,4,2,0:T(8,128)S(1)} fusion(bf16[5,1281,640]{2,1,0:T(8,128)(2,1)} %param.10, bf16[2,640,8,4,5,2]{1,3,5,4,2,0:T(4,128)(2,1)S(1)} %bitcast.127), kind=kOutput, calls=%fused_computation.10 | convolution fusion | flops 1049395200 | bytes 12296960 | tf_op jit(solution)/shard_map/srl,plvcsq->sqpvcr/dot_general | solution.py:44
  248.7 23.4 %all-reduce.2.cloned.1.call-done = f32[8,4,5,1281]{3,0,1,2:T(8,128)} async-done(((f32[8,4,5,1281]{3,0,1,2:T(8,128)}), f32[8,4,5,1281]{3,0,1,2:T(8,128)}) %all-reduce.2.cloned.1.call-update) | async-done | bytes 819856 | tf_op jit(solution)/shard_map/psum | solution.py:117
  274.1 5.1 %fusion.18 = bf16[5,2,2,8,4,640]{5,3,4,2,1,0:T(8,128)(2,1)S(1)} fusion(bf16[5,1281,640]{2,1,0:T(8,128)(2,1)} %param.10, bf16[5,1,2,8,4,1281]{5,3,4,0,2,1:T(8,128)(2,1)S(1)} %maximum_bitcast_fusion.1, bf16[5,1,2,8,4,1281]{5,3,4,0,2,1:T(8,128)(2,1)S(1)} %maximum_bitcast_fusion), kind=kOutput, calls=%fused_computation.16 | convolution fusion | flops 1050624640 | bytes 10657280 | tf_op jit(solution)/shard_map/srl,sqpvcr->plvcsq/dot_general | solution.py:82
  279.5 4.2 all_to_all.70
  283.7 10.7 %copy.87 = bf16[2,2,640,4,4,10]{5,4,3,0,2,1:T(4,128)(2,1)} copy(bf16[2,2,640,4,4,10]{2,4,5,0,3,1:T(4,128)(2,1)S(1)} %bitcast.126) | data formatting | bytes 1638400 | tf_op jit(solution)/shard_map/all_to_all | solution.py:120
  294.4 18.5 %reshape.569 = bf16[128,2,1600]{2,1,0:T(2,128)(2,1)} reshape(bf16[1280,2,4,4,10]{4,3,2,1,0:T(4,128)(2,1)} %bitcast.123) | data formatting | bytes 1638400
  312.9 13.6 %all-to-all-start.3 = ((bf16[128,2,1600]{2,1,0:T(2,128)(2,1)}), bf16[128,2,1600]{2,1,0:T(2,128)(2,1)S(1)}, u32[]{:S(2)}, u32[]{:S(2)}) async-start(bf16[128,2,1600]{2,1,0:T(2,128)(2,1)} %reshape.569), calls=%async_computation.3 | async-start | bytes 1703936 | tf_op jit(solution)/shard_map/all_to_all | solution.py:121
  326.5 26.4 %all-to-all-done.3 = bf16[128,2,1600]{2,1,0:T(2,128)(2,1)S(1)} async-done(((bf16[128,2,1600]{2,1,0:T(2,128)(2,1)}), bf16[128,2,1600]{2,1,0:T(2,128)(2,1)S(1)}, u32[]{:S(2)}, u32[]{:S(2)}) %all-to-all-start.3) | async-done | bytes 819232 | tf_op jit(solution)/shard_map/all_to_all | solution.py:121
  352.9 25.9 %reshape.570 = bf16[1280,2,4,4,10]{4,3,2,1,0:T(4,128)(2,1)} reshape(bf16[128,2,1600]{2,1,0:T(2,128)(2,1)S(1)} %all-to-all-done.3) | data formatting | bytes 1638400
  378.8 20.2 %copy.105 = bf16[2,128,10,4,4,10]{5,1,4,3,2,0:T(8,128)(2,1)} copy(bf16[2,128,10,4,4,10]{5,4,3,0,2,1:T(4,128)(2,1)} %bitcast.124) | data formatting | bytes 1638400 | tf_op jit(solution)/shard_map/all_to_all | solution.py:121
  399.0 17.0 %all_to_all.64 = bf16[2,10,4,4,1280]{4,3,2,1,0:T(4,128)(2,1)S(1)} reshape(bf16[2,10,4,4,128,10]{5,4,3,2,1,0:T(8,128)(2,1)} %bitcast.125) | data formatting | bytes 1638400 | tf_op jit(solution)/shard_map/all_to_all | solution.py:121
  416.1 2.2 fusion.5
  (38 shorter events, 10.1 us)
Async XLA Ops:
  8.3 1.7 copy-start.2
  8.3 1.8 copy-start.1
  41.8 42.3 %all-to-all-start = ((bf16[128,2,1600]{2,1,0:T(2,128)(2,1)}), bf16[128,2,1600]{2,1,0:T(2,128)(2,1)S(1)}, u32[]{:S(2)}, u32[]{:S(2)}) async-start(bf16[128,2,1600]{2,1,0:T(2,128)(2,1)} %reshape.565), calls=%async_computation | async-start | bytes 1703936 | tf_op jit(solution)/shard_map/all_to_all | solution.py:111
  58.1 214.0 %all-reduce.2.cloned.1.call-start = ((), (), s32[]{:S(2)}) async-start(), calls=%async_computation.4 | async-start | bytes 1802240 | tf_op jit(solution)/shard_map/psum | solution.py:117
  247.4 24.7 %copy-start = (f32[8,2]{0,1:T(2,128)S(1)}, f32[8,2]{0,1:T(2,128)}, u32[]{:S(2)}) copy-start(f32[8,2]{0,1:T(2,128)} %param.11) | copy-start | bytes 196
  312.9 40.0 %all-to-all-start.3 = ((bf16[128,2,1600]{2,1,0:T(2,128)(2,1)}), bf16[128,2,1600]{2,1,0:T(2,128)(2,1)S(1)}, u32[]{:S(2)}, u32[]{:S(2)}) async-start(bf16[128,2,1600]{2,1,0:T(2,128)(2,1)} %reshape.569), calls=%async_computation.3 | async-start | bytes 1703936 | tf_op jit(solution)/shard_map/all_to_all | solution.py:121
Sparse Core Ops, SparseCore 0:
  248.7 23.3 all-reduce.1
where the time goes:
time: 436 us; the launch traced here: 427 us
  local copies, waits for them, and re-layouts  274 us (63%)
  waiting for transfers between devices  74.8 us (17%)
  starting transfers between devices  29.9 us (7%)
  matrix products  15.6 us (4%)
  between operations  14.1 us (3%)
  blocking collectives  11.3 us (3%)
  other arithmetic  7.36 us (2%)
    unnamed x12, local copies, waits for them, and re-layouts  147 us
    all_to_all x2, local copies, waits for them, and re-layouts, on_device(): lax.all_to_all(outgoing, 'band', split_axis=4, concat_axis=1, tiled=True)  52.9 us
    all_to_all x2, local copies, waits for them, and re-layouts, on_device(): lax.all_to_all(returning, 'band', split_axis=1, concat_axis=4, tiled=True)  37.2 us
    all_to_all x1, waiting for transfers between devices, on_device(): lax.all_to_all(returning, 'band', split_axis=1, concat_axis=4, tiled=True)  26.4 us
    all_to_all x1, waiting for transfers between devices, on_device(): lax.all_to_all(outgoing, 'band', split_axis=4, concat_axis=1, tiled=True)  25 us
    psum x1, waiting for transfers between devices, on_device(): lax.psum(legendre_forward(arrived, legendre, leading, midpoint), 'lev')  23.4 us
    all_to_all x1, starting transfers between devices, on_device(): lax.all_to_all(outgoing, 'band', split_axis=4, concat_axis=1, tiled=True)  16.3 us
    all_to_all x1, starting transfers between devices, on_device(): lax.all_to_all(returning, 'band', split_axis=1, concat_axis=4, tiled=True)  13.6 us
  transfers between devices with their start and end apart: 3, of which 3 were waited for; matrix products, arithmetic and copies ran while one was open for 0% of the time, Pallas kernels for 0%

commit v1 on v0

v1 whole, which is shorter than its diff:
```python
import functools

import jax
import jax.numpy as jnp
from jax import lax
from jax.experimental import pallas as pl
from jax.experimental.pallas import tpu as pltpu
from jax.sharding import PartitionSpec as P

F32 = jnp.float32
BF16 = jnp.bfloat16
LANES = 128
NT = (((1,), (1,)), ((), ()))
NN = (((1,), (0,)), ((), ()))
VMEM = pl.BlockSpec(memory_space=pltpu.VMEM)
SMEM = pl.BlockSpec(memory_space=pltpu.SMEM)
TILES = 5
ROWS = 26


def dot(a, b, dims):
    return lax.dot_general(a, b, dims, preferred_element_type=F32)


def one_hot_rows(listing, slot, q, orders, bands):
    slots = listing.shape[1] // bands
    where_ = lax.broadcasted_iota(jnp.int32, (bands, listing.shape[1]), 1)
    owner = lax.broadcasted_iota(jnp.int32, (bands, listing.shape[1]), 0)
    lead = jnp.sum(jnp.where(where_ == owner * slots + slot, listing, 0), axis=1, keepdims=True)
    order = lead if q == 0 else orders - 1 - lead
    column = lax.broadcasted_iota(jnp.int32, (bands, orders), 1)
    return jnp.where(column == order, 1.0, 0.0).astype(BF16)


def cutoff_of(points, orders):
    return jnp.minimum(orders - 1, lax.shift_right_arithmetic(points - 1, 1))


def pack_kernel(x_ref, points_ref, weight_ref, listing_ref, out_ref, sel_ref, fold, wide):
    rows, _, levels, comps, orders = x_ref.shape
    bands = sel_ref.shape[0] // (2 * TILES)
    vc = levels * comps
    group = 2 * vc
    column = lax.broadcasted_iota(jnp.int32, (comps, orders), 1)
    for i in range(rows):
        live = (column <= cutoff_of(points_ref[i], orders)).astype(F32)
        factor = live * weight_ref[i]
        for v in range(levels):
            north = x_ref[i, 0, v].astype(F32)
            south = x_ref[i, 1, v].astype(F32)
            fold[pl.ds(i * group + v * comps, comps), :] = (north + south) * factor
            fold[pl.ds(i * group + vc + v * comps, comps), :] = (north - south) * factor
    folded = fold[...].astype(BF16)
    gap = jnp.zeros((64, orders), BF16)
    first = jnp.concatenate([folded, gap], axis=0)
    second = jnp.concatenate([gap, folded[256:], folded[:256]], axis=0)
    listing = listing_ref[...]
    for j in range(TILES):
        sel0 = one_hot_rows(listing, j, 0, orders, bands)
        sel1 = one_hot_rows(listing, j, 1, orders, bands)
        sel_ref[pl.ds((2 * j) * bands, bands), :] = sel0
        sel_ref[pl.ds((2 * j + 1) * bands, bands), :] = sel1
        v0 = dot(sel0, first, NT)
        v1 = dot(sel1, second, NT)
        tiles = [v0[:, :128], v0[:, 128:256], v0[:, 256:] + v1[:, :128], v1[:, 128:256], v1[:, 256:]]
        for t in range(TILES):
            wide[pl.ds(TILES * j + t, bands, stride=ROWS), :] = tiles[t]
    wide[pl.ds(ROWS - 1, bands, stride=ROWS), :] = jnp.zeros((bands, LANES), F32)
    out_ref[...] = wide[...].astype(BF16)


def split_tiles(tiles):
    return (
        jnp.concatenate([tiles[0], tiles[1], tiles[2][:64]], axis=0),
        jnp.concatenate([tiles[3], tiles[4], tiles[2][64:]], axis=0),
    )


def join_tiles(first, second):
    return [
        first[:128],
        first[128:256],
        jnp.concatenate([first[256:], second[256:]], axis=0),
        second[:128],
        second[128:256],
    ]


def transform_kernel(got_ref, own_ref, other_ref, place_ref, order_ref, kappa_ref, out_ref, wide, held, spread):
    slots, nrows, half = own_ref.shape
    orders = nrows - 1
    bands = got_ref.shape[0] // ROWS
    per_band = orders // bands
    levels = kappa_ref.shape[0] // 2
    vc = 4 * levels
    four = 4 * vc
    band = lax.axis_index("band")
    lev = lax.axis_index("lev")
    wide[...] = got_ref[...].astype(F32)
    for j in range(slots):
        tiles = [jnp.transpose(wide[pl.ds(TILES * j + t, bands, stride=ROWS), :]) for t in range(TILES)]
        for q, both in enumerate(split_tiles(tiles)):
            for p in range(2):
                for i in range(per_band):
                    piece = both[i * 2 * vc + p * vc : i * 2 * vc + (p + 1) * vc]
                    held[pl.ds(j * four + (2 * p + q) * vc, vc), pl.ds(i * bands, bands)] = piece.astype(BF16)
    spread[...] = dot(held[...], place_ref[...], NN).astype(BF16)

    which = lax.broadcasted_iota(jnp.int32, (vc, 1), 0)
    kappa = jnp.zeros((vc, 1), F32)
    for n in range(2 * levels):
        kappa = jnp.where(lax.shift_right_logical(which, 1) == n, kappa_ref[lev * levels + n // 2, n % 2], kappa)

    def rows_of(start, count, slot):
        first_order = order_ref[band * slots + slot]
        second_order = orders - 1 - first_order
        row = start + lax.broadcasted_iota(jnp.int32, (1, count), 1)
        odd = row > orders // 2
        odd_number = odd.astype(jnp.int32)
        position = row - odd_number * (orders // 2 + 1)
        boundary = jnp.where(
            odd,
            lax.shift_right_arithmetic(orders - first_order, 1),
            lax.shift_right_arithmetic(orders + 1 - first_order, 1),
        )
        leading = position < boundary
        degree = jnp.where(
            leading,
            first_order + odd_number + 2 * position,
            second_order + odd_number + 2 * (position - boundary),
        )
        growth = (degree * (degree + 1)).astype(F32) / float(orders * (orders + 1))
        return odd, leading, 1.0 / (1.0 + kappa * growth)

    def damp(coeffs, start, count, slot):
        odd, leading, factor = rows_of(start, count, slot)
        parts = [coeffs[n * vc : (n + 1) * vc] for n in range(4)]
        picked = jnp.where(odd, jnp.where(leading, parts[2], parts[3]), jnp.where(leading, parts[0], parts[1]))
        spectral = picked * factor
        masks = [
            jnp.logical_and(jnp.logical_not(odd), leading),
            jnp.logical_not(jnp.logical_or(odd, leading)),
            jnp.logical_and(odd, leading),
            jnp.logical_and(odd, jnp.logical_not(leading)),
        ]
        return jnp.concatenate([jnp.where(m, spectral, 0.0) for m in masks], axis=0).astype(BF16)

    for j in range(slots):
        mine = spread[pl.ds(j * four, four), :]
        mine_a, mine_b = mine[:, :half], mine[:, half:]
        coeffs = dot(mine_a, own_ref[j, :orders, :], NT) + dot(mine_b, other_ref[j, :orders, :], NT)
        last_a = own_ref[j, pl.ds(orders, 1), :].astype(F32)
        last_b = other_ref[j, pl.ds(orders, 1), :].astype(F32)
        last = jnp.sum(mine_a.astype(F32) * last_a, axis=1, keepdims=True) + jnp.sum(
            mine_b.astype(F32) * last_b, axis=1, keepdims=True
        )
        chosen = damp(coeffs, 0, orders, j)
        chosen_last = damp(last, orders, 1, j).astype(F32)
        held[pl.ds(j * four, four), pl.ds(0, half)] = (
            dot(chosen, own_ref[j, :orders, :], NN) + chosen_last * last_a
        ).astype(BF16)
        held[pl.ds(j * four, four), pl.ds(half, half)] = (
            dot(chosen, other_ref[j, :orders, :], NN) + chosen_last * last_b
        ).astype(BF16)
    back = dot(held[...], place_ref[...], NT)
    for j in range(slots):
        pair = []
        for q in range(2):
            pieces = []
            for i in range(per_band):
                for p in range(2):
                    start = j * four + (2 * p + q) * vc
                    pieces.append(back[start : start + vc, i * bands : (i + 1) * bands])
            pair.append(jnp.concatenate(pieces, axis=0))
        for t, tile in enumerate(join_tiles(*pair)):
            wide[pl.ds(TILES * j + t, bands, stride=ROWS), :] = jnp.transpose(tile)
    wide[pl.ds(ROWS - 1, bands, stride=ROWS), :] = jnp.zeros((bands, LANES), F32)
    out_ref[...] = wide[...].astype(BF16)


def unpack_kernel(got_ref, points_ref, sel_ref, out_ref, wide, gathered, placed):
    rows, _, levels, comps, orders = out_ref.shape
    bands = got_ref.shape[0] // ROWS
    vc = levels * comps
    wide[...] = got_ref[...].astype(F32)
    for j in range(TILES):
        tiles = [jnp.transpose(wide[pl.ds(TILES * j + t, bands, stride=ROWS), :]) for t in range(TILES)]
        for q, both in enumerate(split_tiles(tiles)):
            gathered[:, pl.ds((2 * j + q) * bands, bands)] = both.astype(BF16)
    placed[...] = dot(gathered[...], sel_ref[...], NN)
    column = lax.broadcasted_iota(jnp.int32, (comps, orders), 1)
    for i in range(rows):
        live = (column <= cutoff_of(points_ref[i], orders)).astype(F32)
        for v in range(levels):
            even = placed[pl.ds(i * 2 * vc + v * comps, comps), :]
            odd = placed[pl.ds(i * 2 * vc + vc + v * comps, comps), :]
            out_ref[i, 0, v] = ((even + odd) * live).astype(BF16)
            out_ref[i, 1, v] = ((even - odd) * live).astype(BF16)


def kernel_params(mib):
    return pltpu.CompilerParams(vmem_limit_bytes=mib * 1024 * 1024)


def exchange(packed, bands):
    shaped = packed.reshape(bands, ROWS // 2, 2, LANES)
    return lax.all_to_all(shaped, "band", split_axis=0, concat_axis=0, tiled=True).reshape(packed.shape)


def on_device(bands, fourier_in, row_points, gauss_weight, pair_order, legendre, diffusion):
    rows, _, levels, comps, orders = fourier_in.shape
    group = 2 * levels * comps * rows
    message = jax.ShapeDtypeStruct((bands * ROWS, LANES), BF16)
    other = lax.ppermute(legendre, "lev", [(0, 1), (1, 0)])
    packed, selector = pl.pallas_call(
        pack_kernel,
        out_shape=(message, jax.ShapeDtypeStruct((orders, orders), BF16)),
        in_specs=[VMEM, SMEM, SMEM, VMEM],
        out_specs=(VMEM, VMEM),
        scratch_shapes=[pltpu.VMEM((group, orders), F32), pltpu.VMEM((bands * ROWS, LANES), F32)],
        compiler_params=kernel_params(32),
        name="pack",
    )(fourier_in, row_points, gauss_weight, pair_order[None, :])
    arrived = exchange(packed, bands)

    lev = lax.axis_index("lev")
    half = orders // 2
    source = lax.broadcasted_iota(jnp.int32, (orders, orders), 0)
    target = lax.broadcasted_iota(jnp.int32, (orders, orders), 1)
    latitude = (source % bands) * rows + source // bands
    turned = jnp.where(latitude >= half, latitude - half, latitude + half)
    place = (jnp.where(lev == 0, latitude, turned) == target).astype(BF16)

    produced = pl.pallas_call(
        transform_kernel,
        out_shape=message,
        in_specs=[VMEM, VMEM, VMEM, VMEM, SMEM, SMEM],
        out_specs=VMEM,
        scratch_shapes=[
            pltpu.VMEM((bands * ROWS, LANES), F32),
            pltpu.VMEM((group, orders), BF16),
            pltpu.VMEM((group, orders), BF16),
        ],
        compiler_params=kernel_params(56),
        name="transform",
    )(arrived, legendre, other, place, pair_order, diffusion)
    landed = exchange(produced, bands)
    return pl.pallas_call(
        unpack_kernel,
        out_shape=jax.ShapeDtypeStruct(fourier_in.shape, BF16),
        in_specs=[VMEM, SMEM, VMEM],
        out_specs=VMEM,
        scratch_shapes=[
            pltpu.VMEM((bands * ROWS, LANES), F32),
            pltpu.VMEM((group, orders), BF16),
            pltpu.VMEM((group, orders), F32),
        ],
        compiler_params=kernel_params(32),
        name="unpack",
    )(landed, row_points, selector)


def solution(mesh):
    in_specs = (
        P("band", None, "lev", None, None),
        P("band"),
        P("band"),
        P(),
        P("band", None, "lev"),
        P(),
    )
    out_specs = P("band", None, "lev", None, None)
    return jax.shard_map(
        functools.partial(on_device, mesh.shape["band"]),
        mesh=mesh,
        in_specs=in_specs,
        out_specs=out_specs,
        check_vma=False,
    )
```

time: 436 us -> 107 us (0.25); the launches traced: 427 us -> 106 us
  local copies, waits for them, and re-layouts: 274 us -> 5.45 us
  waiting for transfers between devices: 74.8 us -> 21.3 us
  Pallas kernels: 0 us -> 26.3 us
  blocking collectives: 11.3 us -> 31.7 us
  matrix products: 15.6 us -> 0 us
  between operations: 14.1 us -> 0.04 us
  starting transfers between devices: 29.9 us -> 17.7 us
    unnamed x12 -> x11, local copies, waits for them, and re-layouts: 147 us -> 4.76 us
    all_to_all x6 -> x0, local copies, waits for them, and re-layouts: 114 us -> none  [the longest x2 52.9 us: on_device(): lax.all_to_all(outgoing, 'band', split_axis=4, concat_axis=1, tiled=True)]
    all_to_all x2 -> x1, waiting for transfers between devices: 51.4 us -> 21.3 us  [exchange(): lax.all_to_all(shaped, 'band', split_axis=0, concat_axis=0, tiled=True)]
    pallas_call x0 -> x3, Pallas kernels: none -> 26.3 us  [the longest x1 19 us: on_device(): pl.pallas_call(transform_kernel, out_shape=message, in_specs=[VMEM, VMEM,...]
    psum x1 -> x0, waiting for transfers between devices: 23.4 us -> none  [on_device(): lax.psum(legendre_forward(arrived, legendre, leading, midpoint), 'lev')]
    all_to_all x2 -> x1, blocking collectives: 11.3 us -> 31.7 us  [exchange(): lax.all_to_all(shaped, 'band', split_axis=0, concat_axis=0, tiled=True)]
    dot_general x4 -> x0, matrix products: 15.6 us -> none  [the longest x1 6.1 us: legendre_forward(): jnp.einsum('srl,plvcsq->sqpvcr', tables, grouped, preferred_element_type=...]
    all_to_all x2 -> x1, starting transfers between devices: 29.9 us -> 14.4 us  [exchange(): lax.all_to_all(shaped, 'band', split_axis=0, concat_axis=0, tiled=True)]
  transfers between devices with their start and end apart: 3 -> 2, of which waited for: 3 -> 1; matrix products, arithmetic and copies ran while one was open for 0% -> 5% of each run, Pallas kernels for 0% -> 4%
where the time goes in v1:
time: 107 us; the launch traced here: 106 us
  blocking collectives  31.7 us (30%)
  Pallas kernels  26.3 us (25%)
  waiting for transfers between devices  21.3 us (20%)
  starting transfers between devices  17.7 us (17%)
  local copies, waits for them, and re-layouts  5.45 us (5%)
  other arithmetic  3.71 us (3%)
    all_to_all x1, blocking collectives, exchange(): lax.all_to_all(shaped, 'band', split_axis=0, concat_axis=0, tiled=True)  31.7 us
    all_to_all x1, waiting for transfers between devices, exchange(): lax.all_to_all(shaped, 'band', split_axis=0, concat_axis=0, tiled=True)  21.3 us
    pallas_call x1, Pallas kernels, on_device(): pl.pallas_call(transform_kernel, out_shape=message, in_specs=[VMEM, VMEM,...  19 us
    all_to_all x1, starting transfers between devices, exchange(): lax.all_to_all(shaped, 'band', split_axis=0, concat_axis=0, tiled=True)  14.4 us
    unnamed x11, local copies, waits for them, and re-layouts  4.76 us
    pallas_call x1, Pallas kernels, on_device(): pl.pallas_call(pack_kernel, out_shape=(message, jax.ShapeDtypeStruct((ord...  4.24 us
    convert_element_type x1, other arithmetic, on_device(): place = (jnp.where(lev == 0, latitude, turned) == target).astype(BF16)  3.69 us
    ppermute x1, starting transfers between devices, on_device(): other = lax.ppermute(legendre, 'lev', [(0, 1), (1, 0)])  3.24 us
  transfers between devices with their start and end apart: 2, of which 1 were waited for; matrix products, arithmetic and copies ran while one was open for 5% of the time, Pallas kernels for 4%

profile of v1, /device:TPU:1, one launch (start us, length us, event | category | flops | bytes accessed | tf_op | source)
XLA Modules:
  0.0 106.1 jit_solution(14742576718032829714)
XLA Ops:
  0.0 3.2 %collective-permute-start = (bf16[5,1281,640]{2,1,0:T(8,128)(2,1)}, bf16[5,1281,640]{2,1,0:T(8,128)(2,1)}, u32[]{:S(2)}, u32[]{:S(2)}) collective-permute-start(bf16[5,1281,640]{2,1,0:T(8,128)(2,1)} %own_ref.1), channel_id=1, source_target_pairs={{0,1},{1,0},{2,3},{3,2},{4,5},{5,4},{6,7},{7,6},{8,9},{9,8},{10,11... | collective-permute-start | bytes 24595208 | tf_op jit(solution)/shard_map/ppermute | solution.py:214
  3.2 0.7 broadcast_in_dim.3.listing_ref
  3.9 0.0 copy-start.1
  3.9 1.1 %copy-done.1 = bf16[10,2,4,4,1280]{4,3,2,1,0:T(4,128)(2,1)S(1)} copy-done((bf16[10,2,4,4,1280]{4,3,2,1,0:T(4,128)(2,1)S(1)}, bf16[10,2,4,4,1280]{4,3,2,1,0:T(4,128)(2,1)}, u32[]{:S(2)}) %copy-start.1) | copy-done | bytes 819224
  5.1 0.0 copy-start.2
  5.1 0.7 copy-done.2
  5.7 0.0 copy-start.4
  5.7 0.7 copy-done.4
  6.4 4.2 %pack.1 = (bf16[3328,128]{1,0:T(8,128)(2,1)S(1)}, bf16[1280,1280]{1,0:T(8,128)(2,1)S(1)}) custom-call(bf16[10,2,4,4,1280]{4,3,2,1,0:T(4,128)(2,1)S(1)} %copy-done.1, s32[10]{0:T(128)S(1)} %copy-done.2, f32[10]{0:T(128)S(1)} %copy-done.4, s32[1,640]{1,0:T(1,128)S(1)} %broadcast_in_dim.3.listing_ref), custom_call_target="tpu_custom_call" | custom-call | tf_op jit(solution)/shard_map/pack/pallas_call | solution.py:215
  10.6 0.0 copy-start
  10.6 1.0 copy-done
  11.6 14.4 %all-to-all-start = ((bf16[128,13,2,128]{3,2,1,0:T(2,128)(2,1)}), bf16[128,13,2,128]{3,2,1,0:T(2,128)(2,1)}, u32[]{:S(2)}, u32[]{:S(2)}) async-start(bf16[128,13,2,128]{3,2,1,0:T(2,128)(2,1)} %bitcast.5), calls=%async_computation | async-start | bytes 1703936 | tf_op jit(solution)/shard_map/all_to_all | solution.py:207
  26.0 1.3 %copy.7.kappa_ref = f32[8,2]{1,0:T(8,128)} copy(f32[8,2]{0,1:T(2,128)} %param.11) | data formatting | bytes 128 | tf_op args[5]
  27.4 3.7 %fusion.1.place_ref = bf16[1280,1280]{1,0:T(8,128)(2,1)} fusion(s32[1280]{0:T(1024)S(1)} %get-tuple-element.9, s32[1280]{0:T(1024)S(1)} %get-tuple-element.12, s32[1280]{0:T(1024)S(1)} %get-tuple-element.10, s32[1280]{0:T(1024)S(1)} %get-tuple-element.11, pred[1280]{0:T(1024)(128)(4,1)S(1)} %get-tuple-element.13, pred[1280]{0:T(1024)(128)(4,1)S(1)} %get-tuple-element.14, ...), kind=kLoop, calls=%fused_computation.3 | loop fusion | flops 18022400 | bytes 3299841 | tf_op jit(solution)/shard_map/convert_element_type | solution.py:232
  31.1 21.3 %all-to-all-done = bf16[128,13,2,128]{3,2,1,0:T(2,128)(2,1)} async-done(((bf16[128,13,2,128]{3,2,1,0:T(2,128)(2,1)}), bf16[128,13,2,128]{3,2,1,0:T(2,128)(2,1)}, u32[]{:S(2)}, u32[]{:S(2)}) %all-to-all-start) | async-done | bytes 852000 | tf_op jit(solution)/shard_map/all_to_all | solution.py:207
  52.4 0.0 collective-permute-done.other_ref
  52.4 0.0 copy-start.3
  52.4 19.0 %transform.1 = bf16[3328,128]{1,0:T(8,128)(2,1)} custom-call(bf16[3328,128]{1,0:T(8,128)(2,1)} %bitcast.1.got_ref, bf16[5,1281,640]{2,1,0:T(8,128)(2,1)} %own_ref.1, bf16[5,1281,640]{2,1,0:T(8,128)(2,1)} %collective-permute-done.other_ref, bf16[1280,1280]{1,0:T(8,128)(2,1)} %fusion.1.place_ref, s32[640]{0:T(1024)} %order_ref.1, f32[8,2]{1,0:T(8,128)} %copy.7.kappa_ref), custom_call_target="tpu_custom_call" | custom-call | tf_op jit(solution)/shard_map/transform/pallas_call | solution.py:234
  71.4 31.7 %all_to_all.10 = bf16[128,13,2,128]{3,2,1,0:T(2,128)(2,1)S(1)} all-to-all(bf16[128,13,2,128]{3,2,1,0:T(2,128)(2,1)} %bitcast.6), channel_id=1, replica_groups=mesh['band'=128,'lev'=2] {'band'}, dimensions={0} | all-to-all | bytes 1703936 | tf_op jit(solution)/shard_map/all_to_all | solution.py:207
  103.1 0.0 copy-done.3
  103.1 3.0 %unpack.1 = bf16[10,2,4,4,1280]{4,3,2,1,0:T(4,128)(2,1)} custom-call(bf16[3328,128]{1,0:T(8,128)(2,1)S(1)} %bitcast.4, s32[10]{0:T(128)S(1)} %copy-done.3, bf16[1280,1280]{1,0:T(8,128)(2,1)S(1)} %get-tuple-element.8.sel_ref), custom_call_target="tpu_custom_call" | custom-call | tf_op jit(solution)/shard_map/unpack/pallas_call | solution.py:248
  (3 shorter events, 0.0 us)
Async XLA Ops:
  0.0 52.4 %collective-permute-start = (bf16[5,1281,640]{2,1,0:T(8,128)(2,1)}, bf16[5,1281,640]{2,1,0:T(8,128)(2,1)}, u32[]{:S(2)}, u32[]{:S(2)}) collective-permute-start(bf16[5,1281,640]{2,1,0:T(8,128)(2,1)} %own_ref.1), channel_id=1, source_target_pairs={{0,1},{1,0},{2,3},{3,2},{4,5},{5,4},{6,7},{7,6},{8,9},{9,8},{10,11... | collective-permute-start | bytes 24595208 | tf_op jit(solution)/shard_map/ppermute | solution.py:214
  3.9 1.1 %copy-start.1 = (bf16[10,2,4,4,1280]{4,3,2,1,0:T(4,128)(2,1)S(1)}, bf16[10,2,4,4,1280]{4,3,2,1,0:T(4,128)(2,1)}, u32[]{:S(2)}) copy-start(bf16[10,2,4,4,1280]{4,3,2,1,0:T(4,128)(2,1)} %x_ref.1) | copy-start | bytes 2457604
  5.1 0.7 copy-start.2
  5.7 0.7 copy-start.4
  10.6 1.0 copy-start
  11.6 40.8 %all-to-all-start = ((bf16[128,13,2,128]{3,2,1,0:T(2,128)(2,1)}), bf16[128,13,2,128]{3,2,1,0:T(2,128)(2,1)}, u32[]{:S(2)}, u32[]{:S(2)}) async-start(bf16[128,13,2,128]{3,2,1,0:T(2,128)(2,1)} %bitcast.5), calls=%async_computation | async-start | bytes 1703936 | tf_op jit(solution)/shard_map/all_to_all | solution.py:207
  52.4 50.7 %copy-start.3 = (s32[10]{0:T(128)S(1)}, s32[10]{0:T(128)}, u32[]{:S(2)}) copy-start(s32[10]{0:T(128)} %points_ref.3) | copy-start | bytes 124

commit v2 on v1

--- a/solution.py
+++ b/solution.py
@@ -13,6 +13,7 @@
 NT = (((1,), (1,)), ((), ()))
 NN = (((1,), (0,)), ((), ()))
 VMEM = pl.BlockSpec(memory_space=pltpu.VMEM)
+ANY = pl.BlockSpec(memory_space=pl.ANY)
 SMEM = pl.BlockSpec(memory_space=pltpu.SMEM)
 TILES = 5
 ROWS = 26
@@ -36,33 +37,38 @@
     return jnp.minimum(orders - 1, lax.shift_right_arithmetic(points - 1, 1))
 
 
-def pack_kernel(x_ref, points_ref, weight_ref, listing_ref, out_ref, sel_ref, fold, wide):
+def pack_kernel(x_ref, points_ref, weight_ref, listing_ref, out_ref, sel_ref, x_held, fold, wide, x_sem):
     rows, _, levels, comps, orders = x_ref.shape
     bands = sel_ref.shape[0] // (2 * TILES)
     vc = levels * comps
     group = 2 * vc
     column = lax.broadcasted_iota(jnp.int32, (comps, orders), 1)
+    loads = [pltpu.make_async_copy(x_ref.at[i], x_held.at[i], x_sem.at[i]) for i in range(rows)]
+    for load in loads:
+        load.start()
+    listing = listing_ref[...].reshape(1, orders // 2)
+    for q in range(2):
+        for j in range(TILES):
+            sel_ref[pl.ds((q * TILES + j) * bands, bands), :] = one_hot_rows(listing, j, q, orders, bands)
     for i in range(rows):
         live = (column <= cutoff_of(points_ref[i], orders)).astype(F32)
         factor = live * weight_ref[i]
+        loads[i].wait()
         for v in range(levels):
-            north = x_ref[i, 0, v].astype(F32)
-            south = x_ref[i, 1, v].astype(F32)
+            north = x_held[i, 0, v].astype(F32)
+            south = x_held[i, 1, v].astype(F32)
             fold[pl.ds(i * group + v * comps, comps), :] = (north + south) * factor
             fold[pl.ds(i * group + vc + v * comps, comps), :] = (north - south) * factor
     folded = fold[...].astype(BF16)
     gap = jnp.zeros((64, orders), BF16)
     first = jnp.concatenate([folded, gap], axis=0)
     second = jnp.concatenate([gap, folded[256:], folded[:256]], axis=0)
-    listing = listing_ref[...]
+    block = TILES * bands
+    v0 = dot(sel_ref[pl.ds(0, block), :], first, NT)
+    v1 = dot(sel_ref[pl.ds(block, block), :], second, NT)
     for j in range(TILES):
-        sel0 = one_hot_rows(listing, j, 0, orders, bands)
-        sel1 = one_hot_rows(listing, j, 1, orders, bands)
-        sel_ref[pl.ds((2 * j) * bands, bands), :] = sel0
-        sel_ref[pl.ds((2 * j + 1) * bands, bands), :] = sel1
-        v0 = dot(sel0, first, NT)
-        v1 = dot(sel1, second, NT)
-        tiles = [v0[:, :128], v0[:, 128:256], v0[:, 256:] + v1[:, :128], v1[:, 128:256], v1[:, 256:]]
+        a, b = v0[j * bands : (j + 1) * bands], v1[j * bands : (j + 1) * bands]
+        tiles = [a[:, :128], a[:, 128:256], a[:, 256:] + b[:, :128], b[:, 128:256], b[:, 256:]]
         for t in range(TILES):
             wide[pl.ds(TILES * j + t, bands, stride=ROWS), :] = tiles[t]
     wide[pl.ds(ROWS - 1, bands, stride=ROWS), :] = jnp.zeros((bands, LANES), F32)
@@ -186,7 +192,7 @@
     for j in range(TILES):
         tiles = [jnp.transpose(wide[pl.ds(TILES * j + t, bands, stride=ROWS), :]) for t in range(TILES)]
         for q, both in enumerate(split_tiles(tiles)):
-            gathered[:, pl.ds((2 * j + q) * bands, bands)] = both.astype(BF16)
+            gathered[:, pl.ds((q * TILES + j) * bands, bands)] = both.astype(BF16)
     placed[...] = dot(gathered[...], sel_ref[...], NN)
     column = lax.broadcasted_iota(jnp.int32, (comps, orders), 1)
     for i in range(rows):
@@ -215,12 +221,22 @@
     packed, selector = pl.pallas_call(
         pack_kernel,
         out_shape=(message, jax.ShapeDtypeStruct((orders, orders), BF16)),
-        in_specs=[VMEM, SMEM, SMEM, VMEM],
+        in_specs=[ANY, SMEM, SMEM, VMEM],
         out_specs=(VMEM, VMEM),
-        scratch_shapes=[pltpu.VMEM((group, orders), F32), pltpu.VMEM((bands * ROWS, LANES), F32)],
-        compiler_params=kernel_params(32),
+        scratch_shapes=[
+            pltpu.VMEM(fourier_in.shape, BF16),
+            pltpu.VMEM((group, orders), F32),
+            pltpu.VMEM((bands * ROWS, LANES), F32),
+            pltpu.SemaphoreType.DMA((rows,)),
+        ],
+        compiler_params=kernel_params(16),
         name="pack",
-    )(fourier_in, row_points, gauss_weight, pair_order[None, :])
+    )(
+        pltpu.with_memory_space_constraint(fourier_in, pltpu.HBM),
+        pltpu.with_memory_space_constraint(row_points, pltpu.HBM),
+        pltpu.with_memory_space_constraint(gauss_weight, pltpu.HBM),
+        pltpu.with_memory_space_constraint(pair_order, pltpu.HBM),
+    )
     arrived = exchange(packed, bands)
 
     lev = lax.axis_index("lev")
@@ -241,9 +257,16 @@
             pltpu.VMEM((group, orders), BF16),
             pltpu.VMEM((group, orders), BF16),
         ],
-        compiler_params=kernel_params(56),
+        compiler_params=kernel_params(16),
         name="transform",
-    )(arrived, legendre, other, place, pair_order, diffusion)
+    )(
+        arrived,
+        pltpu.with_memory_space_constraint(legendre, pltpu.VMEM),
+        pltpu.with_memory_space_constraint(other, pltpu.VMEM),
+        pltpu.with_memory_space_constraint(place, pltpu.VMEM),
+        pltpu.with_memory_space_constraint(pair_order, pltpu.HBM),
+        pltpu.with_memory_space_constraint(diffusion, pltpu.HBM),
+    )
     landed = exchange(produced, bands)
     return pl.pallas_call(
         unpack_kernel,
@@ -255,9 +278,9 @@
             pltpu.VMEM((group, orders), BF16),
             pltpu.VMEM((group, orders), F32),
         ],
-        compiler_params=kernel_params(32),
+        compiler_params=kernel_params(16),
         name="unpack",
-    )(landed, row_points, selector)
+    )(landed, pltpu.with_memory_space_constraint(row_points, pltpu.HBM), selector)
 
 
 def solution(mesh):

time: 107 us -> 104 us (0.972)
  Pallas kernels: 26.3 us -> 23 us
  other arithmetic: 3.71 us -> 2.11 us
  waiting for transfers between devices: 21.3 us -> 22.9 us
    pallas_call x1, Pallas kernels: 19 us -> 14.9 us  [on_device(): pl.pallas_call(transform_kernel, out_shape=message, in_specs=[VMEM, VMEM,...]
    unnamed x11 -> x7, local copies, waits for them, and re-layouts: 4.76 us -> 6.46 us
    convert_element_type x1, other arithmetic: 3.69 us -> 2.09 us  [on_device(): place = (jnp.where(lev == 0, latitude, turned) == target).astype(BF16)]
    all_to_all x1, waiting for transfers between devices: 21.3 us -> 22.9 us  [exchange(): lax.all_to_all(shaped, 'band', split_axis=0, concat_axis=0, tiled=True)]
  transfers between devices with their start and end apart: 2 -> 2, of which waited for: 1 -> 1; matrix products, arithmetic and copies ran while one was open for 5% -> 3% of each run, Pallas kernels for 4% -> 5%
where the time goes in v2:
time: 104 us; the launch traced here: 103 us
  blocking collectives  30.8 us (30%)
  Pallas kernels  23 us (22%)
  waiting for transfers between devices  22.9 us (22%)
  starting transfers between devices  17.7 us (17%)
  local copies, waits for them, and re-layouts  6.46 us (6%)
  other arithmetic  2.11 us (2%)
    all_to_all x1, blocking collectives, exchange(): lax.all_to_all(shaped, 'band', split_axis=0, concat_axis=0, tiled=True)  30.8 us
    all_to_all x1, waiting for transfers between devices, exchange(): lax.all_to_all(shaped, 'band', split_axis=0, concat_axis=0, tiled=True)  22.9 us
    pallas_call x1, Pallas kernels, on_device(): pl.pallas_call(transform_kernel, out_shape=message, in_specs=[VMEM, VMEM,...  14.9 us
    all_to_all x1, starting transfers between devices, exchange(): lax.all_to_all(shaped, 'band', split_axis=0, concat_axis=0, tiled=True)  14.4 us
    unnamed x7, local copies, waits for them, and re-layouts  6.46 us
    pallas_call x1, Pallas kernels, on_device(): pl.pallas_call(pack_kernel, out_shape=(message, jax.ShapeDtypeStruct((ord...  4.89 us
    ppermute x1, starting transfers between devices, on_device(): other = lax.ppermute(legendre, 'lev', [(0, 1), (1, 0)])  3.24 us
    pallas_call x1, Pallas kernels, on_device(): pl.pallas_call(unpack_kernel, out_shape=jax.ShapeDtypeStruct(fourier_in.s...  3.17 us
  transfers between devices with their start and end apart: 2, of which 1 were waited for; matrix products, arithmetic and copies ran while one was open for 3% of the time, Pallas kernels for 5%

profile of v2, /device:TPU:1, one launch (start us, length us, event | category | flops | bytes accessed | tf_op | source)
XLA Modules:
  0.0 103.0 jit_solution(7159157505610561240)
XLA Ops:
  0.0 3.2 %collective-permute-start = (bf16[5,1281,640]{2,1,0:T(8,128)(2,1)}, bf16[5,1281,640]{2,1,0:T(8,128)(2,1)}, u32[]{:S(2)}, u32[]{:S(2)}) collective-permute-start(bf16[5,1281,640]{2,1,0:T(8,128)(2,1)} %own_ref.1), channel_id=1, source_target_pairs={{0,1},{1,0},{2,3},{3,2},{4,5},{5,4},{6,7},{7,6},{8,9},{9,8},{10,11... | collective-permute-start | bytes 24595208 | tf_op jit(solution)/shard_map/ppermute | solution.py:220
  3.2 4.9 %pack.1 = (bf16[3328,128]{1,0:T(8,128)(2,1)}, bf16[1280,1280]{1,0:T(8,128)(2,1)S(1)}) custom-call(bf16[10,2,4,4,1280]{4,3,2,1,0:T(4,128)(2,1)} %x_ref.1, s32[10]{0:T(128)} %points_ref.3, f32[10]{0:T(128)} %weight_ref.1, s32[640]{0:T(1024)} %order_ref.1), custom_call_target="tpu_custom_call" | custom-call | tf_op jit(solution)/shard_map/pack/pallas_call | solution.py:221
  8.1 0.0 copy-start.1
  8.1 1.8 %copy-done.1 = bf16[1280,1280]{1,0:T(8,128)(2,1)} copy-done((bf16[1280,1280]{1,0:T(8,128)(2,1)}, bf16[1280,1280]{1,0:T(8,128)(2,1)S(1)}, u32[]{:S(2)}) %copy-start.1) | copy-done | bytes 3276824
  9.9 14.4 %all-to-all-start = ((bf16[128,13,2,128]{3,2,1,0:T(2,128)(2,1)}), bf16[128,13,2,128]{3,2,1,0:T(2,128)(2,1)}, u32[]{:S(2)}, u32[]{:S(2)}) async-start(bf16[128,13,2,128]{3,2,1,0:T(2,128)(2,1)} %bitcast), calls=%async_computation | async-start | bytes 1703936 | tf_op jit(solution)/shard_map/all_to_all | solution.py:213
  24.3 1.3 %copy.7.kappa_ref = f32[8,2]{1,0:T(8,128)} copy(f32[8,2]{0,1:T(2,128)} %param.11) | data formatting | bytes 128 | tf_op args[5]
  25.7 2.1 %fusion.1.place_ref = bf16[1280,1280]{1,0:T(8,128)(2,1)S(1)} fusion(s32[1280]{0:T(1024)S(1)} %get-tuple-element.9, s32[1280]{0:T(1024)S(1)} %get-tuple-element.12, s32[1280]{0:T(1024)S(1)} %get-tuple-element.10, s32[1280]{0:T(1024)S(1)} %get-tuple-element.11, pred[1280]{0:T(1024)(128)(4,1)S(1)} %get-tuple-element.13, ...), kind=kLoop, calls=%fused_computation.3 | loop fusion | flops 18022400 | bytes 3299841 | tf_op jit(solution)/shard_map/convert_element_type | solution.py:248
  27.8 22.9 %all-to-all-done = bf16[128,13,2,128]{3,2,1,0:T(2,128)(2,1)} async-done(((bf16[128,13,2,128]{3,2,1,0:T(2,128)(2,1)}), bf16[128,13,2,128]{3,2,1,0:T(2,128)(2,1)}, u32[]{:S(2)}, u32[]{:S(2)}) %all-to-all-start) | async-done | bytes 852000 | tf_op jit(solution)/shard_map/all_to_all | solution.py:213
  50.7 0.0 collective-permute-done.other_ref
  50.7 0.0 copy-start
  50.7 3.3 %copy-done = bf16[5,1281,640]{2,1,0:T(8,128)(2,1)S(1)} copy-done((bf16[5,1281,640]{2,1,0:T(8,128)(2,1)S(1)}, bf16[5,1281,640]{2,1,0:T(8,128)(2,1)}, u32[]{:S(2)}) %copy-start) | copy-done | bytes 8198424
  54.1 0.0 copy-start.2
  54.1 14.9 %transform.1 = bf16[3328,128]{1,0:T(8,128)(2,1)S(1)} custom-call(bf16[3328,128]{1,0:T(8,128)(2,1)} %bitcast.1.got_ref, bf16[5,1281,640]{2,1,0:T(8,128)(2,1)S(1)} %copy-done, bf16[5,1281,640]{2,1,0:T(8,128)(2,1)} %collective-permute-done.other_ref, bf16[1280,1280]{1,0:T(8,128)(2,1)S(1)} %fusion.1.place_ref, s32[640]{0:T(1024)} %order_ref.1, f32[8,2]{1,0:T(8,128)} %copy.7.kappa_ref), custom_call_target="tpu_custom_call" | custom-call | tf_op jit(solution)/shard_map/transform/pallas_call | solution.py:250
  69.0 30.8 %all_to_all.10 = bf16[128,13,2,128]{3,2,1,0:T(2,128)(2,1)S(1)} all-to-all(bf16[128,13,2,128]{3,2,1,0:T(2,128)(2,1)S(1)} %bitcast.5), channel_id=1, replica_groups=mesh['band'=128,'lev'=2] {'band'}, dimensions={0} | all-to-all | bytes 1703936 | tf_op jit(solution)/shard_map/all_to_all | solution.py:213
  99.8 0.0 copy-done.2
  99.8 3.2 %unpack.1 = bf16[10,2,4,4,1280]{4,3,2,1,0:T(4,128)(2,1)} custom-call(bf16[3328,128]{1,0:T(8,128)(2,1)S(1)} %bitcast.4, s32[10]{0:T(128)} %points_ref.3, bf16[1280,1280]{1,0:T(8,128)(2,1)S(1)} %copy-done.2), custom_call_target="tpu_custom_call" | custom-call | tf_op jit(solution)/shard_map/unpack/pallas_call | solution.py:271
  (3 shorter events, 0.0 us)
Async XLA Ops:
  0.0 50.7 %collective-permute-start = (bf16[5,1281,640]{2,1,0:T(8,128)(2,1)}, bf16[5,1281,640]{2,1,0:T(8,128)(2,1)}, u32[]{:S(2)}, u32[]{:S(2)}) collective-permute-start(bf16[5,1281,640]{2,1,0:T(8,128)(2,1)} %own_ref.1), channel_id=1, source_target_pairs={{0,1},{1,0},{2,3},{3,2},{4,5},{5,4},{6,7},{7,6},{8,9},{9,8},{10,11... | collective-permute-start | bytes 24595208 | tf_op jit(solution)/shard_map/ppermute | solution.py:220
  8.1 1.8 %copy-start.1 = (bf16[1280,1280]{1,0:T(8,128)(2,1)}, bf16[1280,1280]{1,0:T(8,128)(2,1)S(1)}, u32[]{:S(2)}) copy-start(bf16[1280,1280]{1,0:T(8,128)(2,1)S(1)} %get-tuple-element.8.sel_ref) | copy-start | bytes 9830404
  9.9 40.8 %all-to-all-start = ((bf16[128,13,2,128]{3,2,1,0:T(2,128)(2,1)}), bf16[128,13,2,128]{3,2,1,0:T(2,128)(2,1)}, u32[]{:S(2)}, u32[]{:S(2)}) async-start(bf16[128,13,2,128]{3,2,1,0:T(2,128)(2,1)} %bitcast), calls=%async_computation | async-start | bytes 1703936 | tf_op jit(solution)/shard_map/all_to_all | solution.py:213
  50.7 3.3 %copy-start = (bf16[5,1281,640]{2,1,0:T(8,128)(2,1)S(1)}, bf16[5,1281,640]{2,1,0:T(8,128)(2,1)}, u32[]{:S(2)}) copy-start(bf16[5,1281,640]{2,1,0:T(8,128)(2,1)} %own_ref.1) | copy-start | bytes 24595204
  54.1 45.7 %copy-start.2 = (bf16[1280,1280]{1,0:T(8,128)(2,1)S(1)}, bf16[1280,1280]{1,0:T(8,128)(2,1)}, u32[]{:S(2)}) copy-start(bf16[1280,1280]{1,0:T(8,128)(2,1)} %copy-done.1) | copy-start | bytes 9830404

commit v3 on v2

v3 whole, which is shorter than its diff:
```python
import functools

import jax
import jax.numpy as jnp
from jax import lax
from jax.experimental import pallas as pl
from jax.experimental.pallas import tpu as pltpu
from jax.sharding import PartitionSpec as P

F32 = jnp.float32
BF16 = jnp.bfloat16
LANES = 128
HALF = LANES // 2
NT = (((1,), (1,)), ((), ()))
NN = (((1,), (0,)), ((), ()))
VMEM = pl.BlockSpec(memory_space=pltpu.VMEM)
SMEM = pl.BlockSpec(memory_space=pltpu.SMEM)
ANY = pl.BlockSpec(memory_space=pl.ANY)
TILES = 5
ROWS = 26


def dot(a, b, dims):
    return lax.dot_general(a, b, dims, preferred_element_type=F32)


def one_hot_rows(listing, slot, q, orders, bands):
    slots = listing.shape[1] // bands
    where_ = lax.broadcasted_iota(jnp.int32, (bands, listing.shape[1]), 1)
    owner = lax.broadcasted_iota(jnp.int32, (bands, listing.shape[1]), 0)
    lead = jnp.sum(jnp.where(where_ == owner * slots + slot, listing, 0), axis=1, keepdims=True)
    order = lead if q == 0 else orders - 1 - lead
    column = lax.broadcasted_iota(jnp.int32, (bands, orders), 1)
    return jnp.where(column == order, 1.0, 0.0).astype(BF16)


def cutoff_of(points, orders):
    return jnp.minimum(orders - 1, lax.shift_right_arithmetic(points - 1, 1))


def message_rows(wide, row, bands):
    return wide.at[pl.ds(row, bands, stride=ROWS), :]


def pack_kernel(
    x_ref, points_ref, weight_ref, listing_ref, out_ref, sel_out, x_held, sel_ref, fold, wide, narrow, x_sem, sel_sem, out_sem
):
    rows, _, levels, comps, orders = x_ref.shape
    bands = sel_ref.shape[0] // (2 * TILES)
    vc = levels * comps
    group = 2 * vc
    column = lax.broadcasted_iota(jnp.int32, (comps, orders), 1)
    loads = [pltpu.make_async_copy(x_ref.at[i], x_held.at[i], x_sem.at[i]) for i in range(rows)]
    for load in loads:
        load.start()
    listing = listing_ref[...].reshape(1, orders // 2)
    for j in range(TILES):
        for q in range(2):
            sel_ref[pl.ds((2 * j + q) * bands, bands), :] = one_hot_rows(listing, j, q, orders, bands)
    keep = pltpu.make_async_copy(sel_ref, sel_out, sel_sem)
    keep.start()
    for i in range(rows):
        live = (column <= cutoff_of(points_ref[i], orders)).astype(F32)
        factor = live * weight_ref[i]
        loads[i].wait()
        for v in range(levels):
            north = x_held[i, 0, v].astype(F32)
            south = x_held[i, 1, v].astype(F32)
            fold[pl.ds(i * group + v * comps, comps), :] = (north + south) * factor
            fold[pl.ds(i * group + vc + v * comps, comps), :] = (north - south) * factor
    folded = fold[...].astype(BF16)
    per_tile = LANES // group
    for tile in range(3):
        first = tile * per_tile
        count = min(per_tile, 2 * TILES - first)
        sent = dot(folded, sel_ref[pl.ds(first * bands, count * bands), :], NT)

        def block(i):
            return [sent[i * group : (i + 1) * group, n * bands : (n + 1) * bands] for n in range(count)]

        for pair in range(rows // 2):
            if tile == 2:
                both = jnp.concatenate(block(2 * pair) + block(2 * pair + 1), axis=0)
                message_rows(wide, TILES * pair + 2, bands)[...] = jnp.transpose(both)
            else:
                for odd in range(2):
                    one = jnp.concatenate(block(2 * pair + odd), axis=0)
                    message_rows(wide, TILES * pair + 3 * odd + tile, bands)[...] = jnp.transpose(one)
    message_rows(wide, ROWS - 1, bands)[...] = jnp.zeros((bands, LANES), F32)
    send_out(wide, narrow, out_ref, out_sem)
    keep.wait()


def send_out(wide, narrow, out_ref, sem):
    parts = sem.shape[0]
    size = narrow.shape[0] // parts
    stores = []
    for n in range(parts):
        piece = pl.ds(n * size, size)
        narrow[piece, :] = wide[piece, :].astype(BF16)
        stores.append(pltpu.make_async_copy(narrow.at[piece], out_ref.at[piece], sem.at[n]))
        stores[-1].start()
    for store in stores:
        store.wait()


def gain_kernel(order_ref, kappa_ref, gain_ref):
    slots = gain_ref.shape[0]
    orders = gain_ref.shape[2] - LANES
    levels = kappa_ref.shape[0] // 2
    vc = 4 * levels
    band = lax.axis_index("band")
    lev = lax.axis_index("lev")
    which = lax.broadcasted_iota(jnp.int32, (vc, 1), 0)
    kappa = jnp.zeros((vc, 1), F32)
    for n in range(2 * levels):
        kappa = jnp.where(lax.shift_right_logical(which, 1) == n, kappa_ref[lev * levels + n // 2, n % 2], kappa)
    row = lax.broadcasted_iota(jnp.int32, (1, gain_ref.shape[2]), 1)
    odd = row > orders // 2
    odd_number = odd.astype(jnp.int32)
    position = row - odd_number * (orders // 2 + 1)
    for j in range(slots):
        first_order = order_ref[band * slots + j]
        second_order = orders - 1 - first_order
        boundary = jnp.where(
            odd,
            lax.shift_right_arithmetic(orders - first_order, 1),
            lax.shift_right_arithmetic(orders + 1 - first_order, 1),
        )
        leading = position < boundary
        degree = jnp.where(
            leading,
            first_order + odd_number + 2 * position,
            second_order + odd_number + 2 * (position - boundary),
        )
        growth = (degree * (degree + 1)).astype(F32) / float(orders * (orders + 1))
        factor = 1.0 / (1.0 + kappa * growth)
        for q in range(2):
            for p in range(2):
                mask = jnp.logical_and(
                    leading if q == 0 else jnp.logical_not(leading), odd if p == 1 else jnp.logical_not(odd)
                )
                gain_ref[j, pl.ds((2 * q + p) * vc, vc), :] = jnp.where(mask, factor, 0.0)


def transform_kernel(
    got_ref, own_ref, other_ref, gain_ref, out_ref, wide, narrow, grid, back, own_held, other_held, own_sem, other_sem, out_sem
):
    slots, nrows, half = own_held.shape
    orders = nrows - 1
    bands = got_ref.shape[0] // ROWS
    rows = orders // bands
    four = gain_ref.shape[1]
    lev = lax.axis_index("lev")
    own_first = pl.multiple_of(lev * half, LANES)
    other_first = pl.multiple_of((1 - lev) * half, LANES)
    loads = []
    for j in range(slots):
        loads.append(
            (
                pltpu.make_async_copy(own_ref.at[j], own_held.at[j], own_sem.at[j]),
                pltpu.make_async_copy(other_ref.at[j], other_held.at[j], other_sem.at[j]),
            )
        )
        for load in loads[j]:
            load.start()

    def latitude(i, tile):
        return grid.at[pl.ds(tile * orders + i, bands, stride=rows), :]

    wide[...] = got_ref[...].astype(F32)
    for pair in range(rows // 2):
        parts = [message_rows(wide, TILES * pair + u, bands)[...] for u in range(TILES)]
        for tile, part in enumerate(parts[:3]):
            latitude(2 * pair, tile)[...] = part
        for tile, part in enumerate([parts[3], parts[4], pltpu.roll(parts[2], HALF, 1)]):
            latitude(2 * pair + 1, tile)[...] = part

    left = lax.broadcasted_iota(jnp.int32, (orders, LANES), 1) < HALF
    for tile in range(3):
        inside = range(2 * tile, min(2 * tile + 2, slots))
        mine_own = grid[pl.ds(tile * orders + own_first, half), :].astype(BF16)
        mine_other = grid[pl.ds(tile * orders + other_first, half), :].astype(BF16)
        coeffs, last, last_rows = [], [], []
        for j in inside:
            for load in loads[j]:
                load.wait()
            coeffs.append(dot(own_held[j, :orders, :], mine_own, NN) + dot(other_held[j, :orders, :], mine_other, NN))
            row_own, row_other = own_held[j, pl.ds(orders, 1), :], other_held[j, pl.ds(orders, 1), :]
            last.append(dot(row_own, mine_own, NN) + dot(row_other, mine_other, NN))
            last_rows.append((row_own.astype(F32), row_other.astype(F32)))
        both = jnp.where(left, coeffs[0], coeffs[1]) if len(coeffs) > 1 else coeffs[0]
        turned = jnp.transpose(both)
        ends = jnp.transpose(jnp.concatenate(last + [jnp.zeros((8 - len(last), LANES), F32)], axis=0))
        for n, j in enumerate(inside):
            mine = slice(n * four, (n + 1) * four)
            chosen = (turned[mine] * gain_ref[j, :, pl.ds(0, orders)]).astype(BF16)
            chosen_last = (ends[mine, n : n + 1] * gain_ref[j, :, pl.ds(orders, 1)]).astype(BF16).astype(F32)
            lines = pl.ds(j * four, four)
            back[lines, pl.ds(own_first, half)] = (
                dot(chosen, own_held[j, :orders, :], NN) + chosen_last * last_rows[n][0]
            )
            back[lines, pl.ds(other_first, half)] = (
                dot(chosen, other_held[j, :orders, :], NN) + chosen_last * last_rows[n][1]
            )
        grid[pl.ds(tile * orders, orders), :] = jnp.transpose(back[pl.ds(tile * LANES, LANES), :])

    left = lax.broadcasted_iota(jnp.int32, (bands, LANES), 1) < HALF
    for pair in range(rows // 2):
        even = [latitude(2 * pair, tile)[...] for tile in range(3)]
        odd = [latitude(2 * pair + 1, tile)[...] for tile in range(3)]
        parts = [even[0], even[1], jnp.where(left, even[2], pltpu.roll(odd[2], HALF, 1)), odd[0], odd[1]]
        for u, part in enumerate(parts):
            message_rows(wide, TILES * pair + u, bands)[...] = part
    message_rows(wide, ROWS - 1, bands)[...] = jnp.zeros((bands, LANES), F32)
    send_out(wide, narrow, out_ref, out_sem)


def unpack_kernel(got_ref, points_ref, sel_ref, out_ref, wide, gathered, placed):
    rows, _, levels, comps, orders = out_ref.shape
    bands = got_ref.shape[0] // ROWS
    vc = levels * comps
    group = 2 * vc
    per_tile = LANES // group
    wide[...] = got_ref[...].astype(F32)
    for pair in range(rows // 2):
        parts = [jnp.transpose(message_rows(wide, TILES * pair + u, bands)[...]).astype(BF16) for u in range(TILES)]
        for odd in range(2):
            tiles = [parts[3 * odd], parts[3 * odd + 1], parts[2][odd * HALF : (odd + 1) * HALF]]
            for n in range(2 * TILES):
                at = (n % per_tile) * group
                gathered[pl.ds((2 * pair + odd) * group, group), pl.ds(n * bands, bands)] = tiles[n // per_tile][
                    at : at + group
                ]
    placed[...] = dot(gathered[...], sel_ref[...], NN)
    column = lax.broadcasted_iota(jnp.int32, (comps, orders), 1)
    for i in range(rows):
        live = (column <= cutoff_of(points_ref[i], orders)).astype(F32)
        for v in range(levels):
            even = placed[pl.ds(i * group + v * comps, comps), :]
            odd = placed[pl.ds(i * group + vc + v * comps, comps), :]
            out_ref[i, 0, v] = ((even + odd) * live).astype(BF16)
            out_ref[i, 1, v] = ((even - odd) * live).astype(BF16)


def kernel_params(mib):
    return pltpu.CompilerParams(vmem_limit_bytes=mib * 1024 * 1024)


def exchange(packed, bands):
    shaped = packed.reshape(bands, ROWS // 2, 2, LANES)
    return lax.all_to_all(shaped, "band", split_axis=0, concat_axis=0, tiled=True).reshape(packed.shape)


def in_hbm(*arrays):
    return [pltpu.with_memory_space_constraint(a, pltpu.HBM) for a in arrays]


def in_vmem(*arrays):
    return [pltpu.with_memory_space_constraint(a, pltpu.VMEM) for a in arrays]


def on_device(bands, fourier_in, row_points, gauss_weight, pair_order, legendre, diffusion):
    rows, _, levels, comps, orders = fourier_in.shape
    slots, nrows, half = legendre.shape
    group = 2 * levels * comps
    size = (bands * ROWS, LANES)
    message = pltpu.HBM(size, BF16)
    other = lax.ppermute(legendre, "lev", [(0, 1), (1, 0)])
    points, weights, listing, kappas = in_hbm(row_points, gauss_weight, pair_order, diffusion)
    packed, selector = pl.pallas_call(
        pack_kernel,
        out_shape=(message, pltpu.HBM((orders, orders), BF16)),
        in_specs=[ANY, SMEM, SMEM, VMEM],
        out_specs=(ANY, ANY),
        scratch_shapes=[
            pltpu.VMEM(fourier_in.shape, BF16),
            pltpu.VMEM((orders, orders), BF16),
            pltpu.VMEM((group * rows, orders), F32),
            pltpu.VMEM(size, F32),
            pltpu.VMEM(size, BF16),
            pltpu.SemaphoreType.DMA((rows,)),
            pltpu.SemaphoreType.DMA(()),
            pltpu.SemaphoreType.DMA((4,)),
        ],
        compiler_params=kernel_params(16),
        name="pack",
    )(*in_hbm(fourier_in), points, weights, listing)
    arrived = exchange(packed, bands)

    gain = pl.pallas_call(
        gain_kernel,
        out_shape=jax.ShapeDtypeStruct((slots, 2 * group, orders + LANES), F32),
        in_specs=[SMEM, SMEM],
        out_specs=VMEM,
        compiler_params=kernel_params(8),
        name="gain",
    )(listing, kappas)

    produced = pl.pallas_call(
        transform_kernel,
        out_shape=message,
        in_specs=[VMEM, ANY, ANY, VMEM],
        out_specs=ANY,
        scratch_shapes=[
            pltpu.VMEM(size, F32),
            pltpu.VMEM(size, BF16),
            pltpu.VMEM((3 * orders, LANES), F32),
            pltpu.VMEM((3 * LANES, orders), F32),
            pltpu.VMEM(legendre.shape, BF16),
            pltpu.VMEM(legendre.shape, BF16),
            pltpu.SemaphoreType.DMA((slots,)),
            pltpu.SemaphoreType.DMA((slots,)),
            pltpu.SemaphoreType.DMA((4,)),
        ],
        compiler_params=kernel_params(40),
        name="transform",
    )(arrived, *in_hbm(legendre, other), gain)
    landed = exchange(produced, bands)
    return pl.pallas_call(
        unpack_kernel,
        out_shape=jax.ShapeDtypeStruct(fourier_in.shape, BF16),
        in_specs=[VMEM, SMEM, VMEM],
        out_specs=VMEM,
        scratch_shapes=[
            pltpu.VMEM(size, F32),
            pltpu.VMEM((group * rows, orders), BF16),
            pltpu.VMEM((group * rows, orders), F32),
        ],
        compiler_params=kernel_params(16),
        name="unpack",
    )(landed, points, *in_vmem(selector))


def solution(mesh):
    in_specs = (
        P("band", None, "lev", None, None),
        P("band"),
        P("band"),
        P(),
        P("band", None, "lev"),
        P(),
    )
    out_specs = P("band", None, "lev", None, None)
    return jax.shard_map(
        functools.partial(on_device, mesh.shape["band"]),
        mesh=mesh,
        in_specs=in_specs,
        out_specs=out_specs,
        check_vma=False,
    )
```

time: 104 us -> 95.8 us (0.921)
  local copies, waits for them, and re-layouts: 6.46 us -> 1.35 us
  Pallas kernels: 23 us -> 20.2 us
  other arithmetic: 2.11 us -> 0 us
  waiting for transfers between devices: 22.9 us -> 24.4 us
    unnamed x7 -> x3, local copies, waits for them, and re-layouts: 6.46 us -> 1.35 us
    pallas_call x2 -> x3, Pallas kernels: 19.8 us -> 17 us  [the longest x1 11.6 us: on_device(): pl.pallas_call(transform_kernel, out_shape=message, in_specs=[VMEM, ANY,...]
    convert_element_type x1 -> x0, other arithmetic: 2.09 us -> none  [on_device(): place = (jnp.where(lev == 0, latitude, turned) == target).astype(BF16)]
    all_to_all x1, waiting for transfers between devices: 22.9 us -> 24.4 us  [exchange(): lax.all_to_all(shaped, 'band', split_axis=0, concat_axis=0, tiled=True)]
  transfers between devices with their start and end apart: 2 -> 2, of which waited for: 1 -> 1; matrix products, arithmetic and copies ran while one was open for 3% -> 1% of each run, Pallas kernels for 5% -> 6%
where the time goes in v3:
time: 95.8 us; the launch traced here: 94.9 us
  blocking collectives  31.7 us (33%)
  waiting for transfers between devices  24.4 us (25%)
  Pallas kernels  20.2 us (21%)
  starting transfers between devices  17.2 us (18%)
  local copies, waits for them, and re-layouts  1.35 us (1%)
    all_to_all x1, blocking collectives, exchange(): lax.all_to_all(shaped, 'band', split_axis=0, concat_axis=0, tiled=True)  31.7 us
    all_to_all x1, waiting for transfers between devices, exchange(): lax.all_to_all(shaped, 'band', split_axis=0, concat_axis=0, tiled=True)  24.4 us
    all_to_all x1, starting transfers between devices, exchange(): lax.all_to_all(shaped, 'band', split_axis=0, concat_axis=0, tiled=True)  14 us
    pallas_call x1, Pallas kernels, on_device(): pl.pallas_call(transform_kernel, out_shape=message, in_specs=[VMEM, ANY,...  11.6 us
    pallas_call x1, Pallas kernels, on_device(): pl.pallas_call(pack_kernel, out_shape=(message, pltpu.HBM((orders, orders...  4.43 us
    ppermute x1, starting transfers between devices, on_device(): other = lax.ppermute(legendre, 'lev', [(0, 1), (1, 0)])  3.24 us
    pallas_call x1, Pallas kernels, on_device(): pl.pallas_call(unpack_kernel, out_shape=jax.ShapeDtypeStruct(fourier_in.s...  3.15 us
  transfers between devices with their start and end apart: 2, of which 1 were waited for; matrix products, arithmetic and copies ran while one was open for 1% of the time, Pallas kernels for 6%

profile of v3, /device:TPU:1, one launch (start us, length us, event | category | flops | bytes accessed | tf_op | source)
XLA Modules:
  0.0 94.9 jit_solution(10919164422901630761)
XLA Ops:
  0.0 3.2 %collective-permute-start = (bf16[5,1281,640]{2,1,0:T(8,128)(2,1)}, bf16[5,1281,640]{2,1,0:T(8,128)(2,1)}, u32[]{:S(2)}, u32[]{:S(2)}) collective-permute-start(bf16[5,1281,640]{2,1,0:T(8,128)(2,1)} %own_ref.1), channel_id=1, source_target_pairs={{0,1},{1,0},{2,3},{3,2},{4,5},{5,4},{6,7},{7,6},{8,9},{9,8},{10,11... | collective-permute-start | bytes 24595208 | tf_op jit(solution)/shard_map/ppermute | solution.py:269
  3.2 4.4 %pack.1 = (bf16[3328,128]{1,0:T(8,128)(2,1)}, bf16[1280,1280]{1,0:T(8,128)(2,1)}) custom-call(bf16[10,2,4,4,1280]{4,3,2,1,0:T(4,128)(2,1)} %x_ref.1, s32[10]{0:T(128)} %points_ref.3, f32[10]{0:T(128)} %weight_ref.1, s32[640]{0:T(1024)} %order_ref.1), custom_call_target="tpu_custom_call" | custom-call | tf_op jit(solution)/shard_map/pack/pallas_call | solution.py:271
  7.7 14.0 %all-to-all-start = ((bf16[128,13,2,128]{3,2,1,0:T(2,128)(2,1)}), bf16[128,13,2,128]{3,2,1,0:T(2,128)(2,1)S(1)}, u32[]{:S(2)}, u32[]{:S(2)}) async-start(bf16[128,13,2,128]{3,2,1,0:T(2,128)(2,1)} %bitcast.7), calls=%async_computation | async-start | bytes 1703936 | tf_op jit(solution)/shard_map/all_to_all | solution.py:252
  21.6 1.3 %copy.7.kappa_ref = f32[8,2]{1,0:T(8,128)} copy(f32[8,2]{0,1:T(2,128)} %param.11) | data formatting | bytes 128 | tf_op args[5]
  23.0 1.0 %gain.1.gain_ref = f32[5,64,1408]{2,1,0:T(8,128)S(1)} custom-call(s32[640]{0:T(1024)} %order_ref.1, f32[8,2]{1,0:T(8,128)} %copy.7.kappa_ref), custom_call_target="tpu_custom_call" | custom-call | tf_op jit(solution)/shard_map/gain/pallas_call | solution.py:291
  24.0 24.4 %all-to-all-done = bf16[128,13,2,128]{3,2,1,0:T(2,128)(2,1)S(1)} async-done(((bf16[128,13,2,128]{3,2,1,0:T(2,128)(2,1)}), bf16[128,13,2,128]{3,2,1,0:T(2,128)(2,1)S(1)}, u32[]{:S(2)}, u32[]{:S(2)}) %all-to-all-start) | async-done | bytes 852000 | tf_op jit(solution)/shard_map/all_to_all | solution.py:252
  48.4 0.0 collective-permute-done.other_ref
  48.4 0.0 copy-start
  48.4 11.6 %transform.1 = bf16[3328,128]{1,0:T(8,128)(2,1)} custom-call(bf16[3328,128]{1,0:T(8,128)(2,1)S(1)} %bitcast.5, bf16[5,1281,640]{2,1,0:T(8,128)(2,1)} %own_ref.1, bf16[5,1281,640]{2,1,0:T(8,128)(2,1)} %collective-permute-done.other_ref, f32[5,64,1408]{2,1,0:T(8,128)S(1)} %gain.1.gain_ref), custom_call_target="tpu_custom_call" | custom-call | tf_op jit(solution)/shard_map/transform/pallas_call | solution.py:300
  60.0 31.7 %all_to_all.10 = bf16[128,13,2,128]{3,2,1,0:T(2,128)(2,1)S(1)} all-to-all(bf16[128,13,2,128]{3,2,1,0:T(2,128)(2,1)} %bitcast.6), channel_id=1, replica_groups=mesh['band'=128,'lev'=2] {'band'}, dimensions={0} | all-to-all | bytes 1703936 | tf_op jit(solution)/shard_map/all_to_all | solution.py:252
  91.7 0.0 copy-done
  91.7 3.1 %unpack.1 = bf16[10,2,4,4,1280]{4,3,2,1,0:T(4,128)(2,1)} custom-call(bf16[3328,128]{1,0:T(8,128)(2,1)S(1)} %bitcast.4, s32[10]{0:T(128)} %points_ref.3, bf16[1280,1280]{1,0:T(8,128)(2,1)S(1)} %copy-done), custom_call_target="tpu_custom_call" | custom-call | tf_op jit(solution)/shard_map/unpack/pallas_call | solution.py:320
Async XLA Ops:
  0.0 48.4 %collective-permute-start = (bf16[5,1281,640]{2,1,0:T(8,128)(2,1)}, bf16[5,1281,640]{2,1,0:T(8,128)(2,1)}, u32[]{:S(2)}, u32[]{:S(2)}) collective-permute-start(bf16[5,1281,640]{2,1,0:T(8,128)(2,1)} %own_ref.1), channel_id=1, source_target_pairs={{0,1},{1,0},{2,3},{3,2},{4,5},{5,4},{6,7},{7,6},{8,9},{9,8},{10,11... | collective-permute-start | bytes 24595208 | tf_op jit(solution)/shard_map/ppermute | solution.py:269
  7.7 40.7 %all-to-all-start = ((bf16[128,13,2,128]{3,2,1,0:T(2,128)(2,1)}), bf16[128,13,2,128]{3,2,1,0:T(2,128)(2,1)S(1)}, u32[]{:S(2)}, u32[]{:S(2)}) async-start(bf16[128,13,2,128]{3,2,1,0:T(2,128)(2,1)} %bitcast.7), calls=%async_computation | async-start | bytes 1703936 | tf_op jit(solution)/shard_map/all_to_all | solution.py:252
  48.4 43.3 %copy-start = (bf16[1280,1280]{1,0:T(8,128)(2,1)S(1)}, bf16[1280,1280]{1,0:T(8,128)(2,1)}, u32[]{:S(2)}) copy-start(bf16[1280,1280]{1,0:T(8,128)(2,1)} %get-tuple-element.8.sel_ref) | copy-start | bytes 9830404

commit v4 on v3

v4 whole, which is shorter than its diff:
```python
import functools

import jax
import jax.numpy as jnp
from jax import lax
from jax.experimental import pallas as pl
from jax.experimental.pallas import tpu as pltpu
from jax.sharding import PartitionSpec as P

F32 = jnp.float32
BF16 = jnp.bfloat16
LANES = 128
HALF = LANES // 2
NT = (((1,), (1,)), ((), ()))
NN = (((1,), (0,)), ((), ()))
VMEM = pl.BlockSpec(memory_space=pltpu.VMEM)
SMEM = pl.BlockSpec(memory_space=pltpu.SMEM)
ANY = pl.BlockSpec(memory_space=pl.ANY)
TILES = 5
ROWS = 26


def dot(a, b, dims):
    return lax.dot_general(a, b, dims, preferred_element_type=F32)


def one_hot_rows(listing, slot, q, orders, bands):
    slots = listing.shape[1] // bands
    where_ = lax.broadcasted_iota(jnp.int32, (bands, listing.shape[1]), 1)
    owner = lax.broadcasted_iota(jnp.int32, (bands, listing.shape[1]), 0)
    lead = jnp.sum(jnp.where(where_ == owner * slots + slot, listing, 0), axis=1, keepdims=True)
    order = lead if q == 0 else orders - 1 - lead
    column = lax.broadcasted_iota(jnp.int32, (bands, orders), 1)
    return jnp.where(column == order, 1.0, 0.0).astype(BF16)


def cutoff_of(points, orders):
    return jnp.minimum(orders - 1, lax.shift_right_arithmetic(points - 1, 1))


def message_rows(wide, row, bands):
    return wide.at[pl.ds(row, bands, stride=ROWS), :]


def one_hot(listing_ref, sel_ref):
    orders = sel_ref.shape[1]
    bands = orders // (2 * TILES)
    listing = listing_ref[...].reshape(1, orders // 2)
    for j in range(TILES):
        for q in range(2):
            sel_ref[pl.ds((2 * j + q) * bands, bands), :] = one_hot_rows(listing, j, q, orders, bands)


def pack_kernel(x_ref, points_ref, weight_ref, listing_ref, out_ref, x_held, sel_ref, fold, wide, narrow, x_sem, out_sem):
    rows, _, levels, comps, orders = x_ref.shape
    bands = sel_ref.shape[0] // (2 * TILES)
    vc = levels * comps
    group = 2 * vc
    column = lax.broadcasted_iota(jnp.int32, (comps, orders), 1)
    loads = [pltpu.make_async_copy(x_ref.at[i], x_held.at[i], x_sem.at[i]) for i in range(rows)]
    for load in loads:
        load.start()
    one_hot(listing_ref, sel_ref)
    for i in range(rows):
        live = (column <= cutoff_of(points_ref[i], orders)).astype(F32)
        factor = live * weight_ref[i]
        loads[i].wait()
        for v in range(levels):
            north = x_held[i, 0, v].astype(F32)
            south = x_held[i, 1, v].astype(F32)
            fold[pl.ds(i * group + v * comps, comps), :] = (north + south) * factor
            fold[pl.ds(i * group + vc + v * comps, comps), :] = (north - south) * factor
    folded = fold[...].astype(BF16)
    per_tile = LANES // group
    for tile in range(3):
        first = tile * per_tile
        count = min(per_tile, 2 * TILES - first)
        sent = dot(folded, sel_ref[pl.ds(first * bands, count * bands), :], NT)

        def block(i):
            return [sent[i * group : (i + 1) * group, n * bands : (n + 1) * bands] for n in range(count)]

        for pair in range(rows // 2):
            if tile == 2:
                both = jnp.concatenate(block(2 * pair) + block(2 * pair + 1), axis=0)
                message_rows(wide, TILES * pair + 2, bands)[...] = jnp.transpose(both)
            else:
                for odd in range(2):
                    one = jnp.concatenate(block(2 * pair + odd), axis=0)
                    message_rows(wide, TILES * pair + 3 * odd + tile, bands)[...] = jnp.transpose(one)
    message_rows(wide, ROWS - 1, bands)[...] = jnp.zeros((bands, LANES), F32)
    send_out(wide, narrow, out_ref, out_sem)


def send_out(wide, narrow, out_ref, sem):
    parts = sem.shape[0]
    size = narrow.shape[0] // parts
    stores = []
    for n in range(parts):
        piece = pl.ds(n * size, size)
        narrow[piece, :] = wide[piece, :].astype(BF16)
        stores.append(pltpu.make_async_copy(narrow.at[piece], out_ref.at[piece], sem.at[n]))
        stores[-1].start()
    for store in stores:
        store.wait()


def between_kernel(order_ref, kappa_ref, listing_ref, gain_ref, sel_out, sel_ref, sel_sem):
    one_hot(listing_ref, sel_ref)
    keep = pltpu.make_async_copy(sel_ref, sel_out, sel_sem)
    keep.start()
    slots = gain_ref.shape[0]
    orders = gain_ref.shape[2] - LANES
    levels = kappa_ref.shape[1] // 2
    vc = 4 * levels
    band = lax.axis_index("band")
    lev = lax.axis_index("lev")
    which = lax.broadcasted_iota(jnp.int32, (vc, 1), 0)
    kappa = jnp.zeros((vc, 1), F32)
    for n in range(2 * levels):
        kappa = jnp.where(lax.shift_right_logical(which, 1) == n, kappa_ref[n % 2, lev * levels + n // 2], kappa)
    row = lax.broadcasted_iota(jnp.int32, (1, gain_ref.shape[2]), 1)
    odd = row > orders // 2
    odd_number = odd.astype(jnp.int32)
    position = row - odd_number * (orders // 2 + 1)
    for j in range(slots):
        first_order = order_ref[band * slots + j]
        second_order = orders - 1 - first_order
        boundary = jnp.where(
            odd,
            lax.shift_right_arithmetic(orders - first_order, 1),
            lax.shift_right_arithmetic(orders + 1 - first_order, 1),
        )
        leading = position < boundary
        degree = jnp.where(
            leading,
            first_order + odd_number + 2 * position,
            second_order + odd_number + 2 * (position - boundary),
        )
        growth = (degree * (degree + 1)).astype(F32) / float(orders * (orders + 1))
        factor = 1.0 / (1.0 + kappa * growth)
        for q in range(2):
            for p in range(2):
                mask = jnp.logical_and(
                    leading if q == 0 else jnp.logical_not(leading), odd if p == 1 else jnp.logical_not(odd)
                )
                gain_ref[j, pl.ds((2 * q + p) * vc, vc), :] = jnp.where(mask, factor, 0.0)
    keep.wait()


def transform_kernel(
    got_ref, own_ref, other_ref, gain_ref, out_ref, wide, grid, back, own_held, other_held, own_sem, other_sem
):
    slots, nrows, half = own_held.shape
    orders = nrows - 1
    bands = got_ref.shape[0] // ROWS
    rows = orders // bands
    four = gain_ref.shape[1]
    lev = lax.axis_index("lev")
    own_first = pl.multiple_of(lev * half, LANES)
    other_first = pl.multiple_of((1 - lev) * half, LANES)
    middle = orders // 2
    pieces = [pl.ds(0, middle), pl.ds(middle, nrows - middle)]
    loads = {}
    for j in [slots - 1] + list(range(slots - 1)):
        loads[j] = []
        for n, piece in enumerate(pieces):
            own_load = pltpu.make_async_copy(own_ref.at[j, piece], own_held.at[j, piece], own_sem.at[j, n])
            other_load = pltpu.make_async_copy(other_ref.at[j, piece], other_held.at[j, piece], other_sem.at[j, n])
            loads[j].append((own_load, other_load))

    def start(j):
        for both in loads[j]:
            for load in both:
                load.start()

    start(4)

    def latitude(i, tile):
        return grid.at[pl.ds(tile * orders + i, bands, stride=rows), :]

    wide[...] = got_ref[...].astype(F32)
    right = lax.broadcasted_iota(jnp.int32, (bands, LANES), 1) >= HALF
    second = lax.broadcasted_iota(jnp.int32, (orders, LANES), 1) >= HALF
    columns, coeffs, ends, chosen, chosen_last = {}, {}, {}, {}, {}

    def arrange(tile):
        for pair in range(rows // 2):
            for odd in range(2):
                part = message_rows(wide, TILES * pair + (2 if tile == 2 else 3 * odd + tile), bands)[...]
                latitude(2 * pair + odd, tile)[...] = pltpu.roll(part, HALF, 1) if tile == 2 and odd else part
        columns[tile] = [
            grid[pl.ds(tile * orders + first, half), :].astype(BF16) for first in (own_first, other_first)
        ]

    def forward(j):
        own, other = columns[j // 2]
        parts = []
        for n in range(2):
            for load in loads[j][n]:
                load.wait()
            piece = pl.ds(n * middle, middle)
            parts.append(dot(own_held[j, piece, :], own, NN) + dot(other_held[j, piece, :], other, NN))
        coeffs[j] = jnp.concatenate(parts, axis=0)
        ends[j] = dot(own_held[j, pl.ds(orders, 1), :], own, NN) + dot(other_held[j, pl.ds(orders, 1), :], other, NN)

    def settle(tile):
        inside = [j for j in (2 * tile, 2 * tile + 1) if j < slots]
        both = coeffs[inside[0]] if len(inside) == 1 else jnp.where(second, coeffs[inside[1]], coeffs[inside[0]])
        turned = jnp.transpose(both)
        rest = jnp.zeros((8 - len(inside), LANES), F32)
        turned_ends = jnp.transpose(jnp.concatenate([ends[j] for j in inside] + [rest], axis=0))
        for n, j in enumerate(inside):
            mine = slice(n * four, (n + 1) * four)
            chosen[j] = (turned[mine] * gain_ref[j, :, pl.ds(0, orders)]).astype(BF16)
            chosen_last[j] = (turned_ends[mine, n : n + 1] * gain_ref[j, :, pl.ds(orders, 1)]).astype(BF16).astype(F32)

    def inverse(j):
        for held, first in ((own_held, own_first), (other_held, other_first)):
            back[pl.ds(j * four, four), pl.ds(first, half)] = dot(chosen[j], held[j, :orders, :], NN) + chosen_last[
                j
            ] * held[j, pl.ds(orders, 1), :].astype(F32)

    def finish(tile):
        grid[pl.ds(tile * orders, orders), :] = jnp.transpose(back[pl.ds(tile * LANES, LANES), :])
        for pair in range(rows // 2):
            even, odd = latitude(2 * pair, tile)[...], latitude(2 * pair + 1, tile)[...]
            if tile == 2:
                both = jnp.where(right, pltpu.roll(odd, HALF, 1), even)
                message_rows(wide, TILES * pair + 2, bands)[...] = both
            else:
                message_rows(wide, TILES * pair + tile, bands)[...] = even
                message_rows(wide, TILES * pair + 3 + tile, bands)[...] = odd

    arrange(2)
    start(0)
    arrange(0)
    forward(4)
    start(1)
    forward(0)
    start(2)
    settle(2)
    inverse(4)
    forward(1)
    start(3)
    arrange(1)
    finish(2)
    forward(2)
    settle(0)
    inverse(0)
    forward(3)
    inverse(1)
    finish(0)
    settle(1)
    inverse(2)
    inverse(3)
    finish(1)
    message_rows(wide, ROWS - 1, bands)[...] = jnp.zeros((bands, LANES), F32)
    out_ref[...] = wide[...].astype(BF16)


def unpack_kernel(got_ref, points_ref, sel_ref, out_ref, wide, gathered, placed, held, out_sem):
    rows, _, levels, comps, orders = out_ref.shape
    bands = got_ref.shape[0] // ROWS
    vc = levels * comps
    group = 2 * vc
    per_tile = LANES // group
    wide[...] = got_ref[...].astype(F32)
    for pair in range(rows // 2):
        parts = [jnp.transpose(message_rows(wide, TILES * pair + u, bands)[...]).astype(BF16) for u in range(TILES)]
        for odd in range(2):
            tiles = [parts[3 * odd], parts[3 * odd + 1], parts[2][odd * HALF : (odd + 1) * HALF]]
            for n in range(2 * TILES):
                at = (n % per_tile) * group
                gathered[pl.ds((2 * pair + odd) * group, group), pl.ds(n * bands, bands)] = tiles[n // per_tile][
                    at : at + group
                ]
    width = 2 * LANES
    stores = []
    for n in range(orders // width):
        block = pl.ds(n * width, width)
        placed[:, block] = dot(gathered[...], sel_ref[:, block], NN)
        column = n * width + lax.broadcasted_iota(jnp.int32, (comps, width), 1)
        for i in range(rows):
            live = (column <= cutoff_of(points_ref[i], orders)).astype(F32)
            for v in range(levels):
                even = placed[pl.ds(i * group + v * comps, comps), block]
                odd = placed[pl.ds(i * group + vc + v * comps, comps), block]
                held[i, 0, v, :, block] = ((even + odd) * live).astype(BF16)
                held[i, 1, v, :, block] = ((even - odd) * live).astype(BF16)
        stores.append(
            pltpu.make_async_copy(held.at[:, :, :, :, block], out_ref.at[:, :, :, :, block], out_sem.at[n])
        )
        stores[-1].start()
    for store in stores:
        store.wait()


def kernel_params(mib):
    return pltpu.CompilerParams(vmem_limit_bytes=mib * 1024 * 1024)


def exchange(packed, bands):
    shaped = packed.reshape(bands, ROWS // 2, 2, LANES)
    return lax.all_to_all(shaped, "band", split_axis=0, concat_axis=0, tiled=True).reshape(packed.shape)


def in_hbm(*arrays):
    return [pltpu.with_memory_space_constraint(a, pltpu.HBM) for a in arrays]


def in_vmem(*arrays):
    return [pltpu.with_memory_space_constraint(a, pltpu.VMEM) for a in arrays]


def on_device(bands, fourier_in, row_points, gauss_weight, pair_order, legendre, diffusion):
    rows, _, levels, comps, orders = fourier_in.shape
    slots, nrows, half = legendre.shape
    group = 2 * levels * comps
    size = (bands * ROWS, LANES)
    message = pltpu.HBM(size, BF16)
    other = lax.ppermute(legendre, "lev", [(0, 1), (1, 0)])
    points, weights, listing, kappas = in_hbm(row_points, gauss_weight, pair_order, diffusion.T)
    packed = pl.pallas_call(
        pack_kernel,
        out_shape=message,
        in_specs=[ANY, SMEM, SMEM, VMEM],
        out_specs=ANY,
        scratch_shapes=[
            pltpu.VMEM(fourier_in.shape, BF16),
            pltpu.VMEM((orders, orders), BF16),
            pltpu.VMEM((group * rows, orders), F32),
            pltpu.VMEM(size, F32),
            pltpu.VMEM(size, BF16),
            pltpu.SemaphoreType.DMA((rows,)),
            pltpu.SemaphoreType.DMA((4,)),
        ],
        compiler_params=kernel_params(16),
        name="pack",
    )(*in_hbm(fourier_in), points, weights, listing)
    arrived = exchange(packed, bands)

    gain, selector = pl.pallas_call(
        between_kernel,
        out_shape=(
            jax.ShapeDtypeStruct((slots, 2 * group, orders + LANES), F32),
            pltpu.HBM((orders, orders), BF16),
        ),
        in_specs=[SMEM, SMEM, VMEM],
        out_specs=(VMEM, ANY),
        scratch_shapes=[pltpu.VMEM((orders, orders), BF16), pltpu.SemaphoreType.DMA(())],
        compiler_params=kernel_params(16),
        name="between",
    )(listing, kappas, listing)

    produced = pl.pallas_call(
        transform_kernel,
        out_shape=jax.ShapeDtypeStruct(size, BF16),
        in_specs=[VMEM, ANY, ANY, VMEM],
        out_specs=VMEM,
        scratch_shapes=[
            pltpu.VMEM(size, F32),
            pltpu.VMEM((3 * orders, LANES), F32),
            pltpu.VMEM((3 * LANES, orders), F32),
            pltpu.VMEM(legendre.shape, BF16),
            pltpu.VMEM(legendre.shape, BF16),
            pltpu.SemaphoreType.DMA((slots, 2)),
            pltpu.SemaphoreType.DMA((slots, 2)),
        ],
        compiler_params=kernel_params(40),
        name="transform",
    )(arrived, *in_hbm(legendre, other), gain)
    landed = exchange(produced, bands)
    return pl.pallas_call(
        unpack_kernel,
        out_shape=jax.ShapeDtypeStruct(fourier_in.shape, BF16),
        in_specs=[VMEM, SMEM, VMEM],
        out_specs=ANY,
        scratch_shapes=[
            pltpu.VMEM(size, F32),
            pltpu.VMEM((group * rows, orders), BF16),
            pltpu.VMEM((group * rows, orders), F32),
            pltpu.VMEM(fourier_in.shape, BF16),
            pltpu.SemaphoreType.DMA((orders // (2 * LANES),)),
        ],
        compiler_params=kernel_params(16),
        name="unpack",
    )(landed, points, *in_vmem(selector))


def solution(mesh):
    in_specs = (
        P("band", None, "lev", None, None),
        P("band"),
        P("band"),
        P(),
        P("band", None, "lev"),
        P(),
    )
    out_specs = P("band", None, "lev", None, None)
    return jax.shard_map(
        functools.partial(on_device, mesh.shape["band"]),
        mesh=mesh,
        in_specs=in_specs,
        out_specs=out_specs,
        check_vma=False,
    )
```

time: 95.8 us -> 94.2 us (0.983)
  Pallas kernels: 20.2 us -> 22.2 us
  waiting for transfers between devices: 24.4 us -> 23 us
  local copies, waits for them, and re-layouts: 1.35 us -> 0.01 us
    pallas_call x3, Pallas kernels: 17 us -> 19.1 us  [the longest x1 10.8 us: on_device(): pl.pallas_call(transform_kernel, out_shape=jax.ShapeDtypeStruct(size, BF1...]
    all_to_all x1, waiting for transfers between devices: 24.4 us -> 23 us  [exchange(): lax.all_to_all(shaped, 'band', split_axis=0, concat_axis=0, tiled=True)]
    unnamed x3 -> x2, local copies, waits for them, and re-layouts: 1.35 us -> 0.01 us
  transfers between devices with their start and end apart: 2 -> 2, of which waited for: 1 -> 1; matrix products, arithmetic and copies ran while one was open for 1% -> 0% of each run, Pallas kernels for 6% -> 9%
where the time goes in v4:
time: 94.2 us; the launch traced here: 93.3 us
  blocking collectives  30.8 us (33%)
  waiting for transfers between devices  23 us (24%)
  Pallas kernels  22.2 us (24%)
  starting transfers between devices  17.2 us (18%)
    all_to_all x1, blocking collectives, exchange(): lax.all_to_all(shaped, 'band', split_axis=0, concat_axis=0, tiled=True)  30.8 us
    all_to_all x1, waiting for transfers between devices, exchange(): lax.all_to_all(shaped, 'band', split_axis=0, concat_axis=0, tiled=True)  23 us
    all_to_all x1, starting transfers between devices, exchange(): lax.all_to_all(shaped, 'band', split_axis=0, concat_axis=0, tiled=True)  14 us
    pallas_call x1, Pallas kernels, on_device(): pl.pallas_call(transform_kernel, out_shape=jax.ShapeDtypeStruct(size, BF1...  10.8 us
    pallas_call x1, Pallas kernels, on_device(): pl.pallas_call(pack_kernel, out_shape=message, in_specs=[ANY, SMEM, SMEM,...  4.53 us
    pallas_call x1, Pallas kernels, on_device(): pl.pallas_call(between_kernel, out_shape=(jax.ShapeDtypeStruct((slots, 2...  3.78 us
    ppermute x1, starting transfers between devices, on_device(): other = lax.ppermute(legendre, 'lev', [(0, 1), (1, 0)])  3.24 us
    pallas_call x1, Pallas kernels, on_device(): pl.pallas_call(unpack_kernel, out_shape=jax.ShapeDtypeStruct(fourier_in.s...  3.06 us
  transfers between devices with their start and end apart: 2, of which 1 were waited for; matrix products, arithmetic and copies ran while one was open for 0% of the time, Pallas kernels for 9%

profile of v4, /device:TPU:1, one launch (start us, length us, event | category | flops | bytes accessed | tf_op | source)
XLA Modules:
  0.0 93.3 jit_solution(6664734428577098313)
XLA Ops:
  0.0 3.2 %collective-permute-start = (bf16[5,1281,640]{2,1,0:T(8,128)(2,1)}, bf16[5,1281,640]{2,1,0:T(8,128)(2,1)}, u32[]{:S(2)}, u32[]{:S(2)}) collective-permute-start(bf16[5,1281,640]{2,1,0:T(8,128)(2,1)} %own_ref.1), channel_id=1, source_target_pairs={{0,1},{1,0},{2,3},{3,2},{4,5},{5,4},{6,7},{7,6},{8,9},{9,8},{10,11... | collective-permute-start | bytes 24595208 | tf_op jit(solution)/shard_map/ppermute | solution.py:322
  3.2 4.5 %pack.1 = bf16[3328,128]{1,0:T(8,128)(2,1)} custom-call(bf16[10,2,4,4,1280]{4,3,2,1,0:T(4,128)(2,1)} %x_ref.1, s32[10]{0:T(128)} %points_ref.3, f32[10]{0:T(128)} %weight_ref.1, s32[640]{0:T(1024)} %listing_ref.3), custom_call_target="tpu_custom_call" | custom-call | tf_op jit(solution)/shard_map/pack/pallas_call | solution.py:324
  7.8 14.0 %all-to-all-start = ((bf16[128,13,2,128]{3,2,1,0:T(2,128)(2,1)}), bf16[128,13,2,128]{3,2,1,0:T(2,128)(2,1)S(1)}, u32[]{:S(2)}, u32[]{:S(2)}) async-start(bf16[128,13,2,128]{3,2,1,0:T(2,128)(2,1)} %bitcast.8), calls=%async_computation | async-start | bytes 1703936 | tf_op jit(solution)/shard_map/all_to_all | solution.py:305
  21.8 3.8 %between.1 = (f32[5,64,1408]{2,1,0:T(8,128)S(1)}, bf16[1280,1280]{1,0:T(8,128)(2,1)}) custom-call(s32[640]{0:T(1024)} %listing_ref.3, f32[2,8]{1,0:T(2,128)} %bitcast.9, s32[640]{0:T(1024)} %listing_ref.3), custom_call_target="tpu_custom_call" | custom-call | tf_op jit(solution)/shard_map/between/pallas_call | solution.py:343
  25.5 23.0 %all-to-all-done = bf16[128,13,2,128]{3,2,1,0:T(2,128)(2,1)S(1)} async-done(((bf16[128,13,2,128]{3,2,1,0:T(2,128)(2,1)}), bf16[128,13,2,128]{3,2,1,0:T(2,128)(2,1)S(1)}, u32[]{:S(2)}, u32[]{:S(2)}) %all-to-all-start) | async-done | bytes 852000 | tf_op jit(solution)/shard_map/all_to_all | solution.py:305
  48.5 0.0 collective-permute-done.other_ref
  48.5 0.0 copy-start
  48.5 10.8 %transform.1 = bf16[3328,128]{1,0:T(8,128)(2,1)S(1)} custom-call(bf16[3328,128]{1,0:T(8,128)(2,1)S(1)} %bitcast.6, bf16[5,1281,640]{2,1,0:T(8,128)(2,1)} %own_ref.1, bf16[5,1281,640]{2,1,0:T(8,128)(2,1)} %collective-permute-done.other_ref, f32[5,64,1408]{2,1,0:T(8,128)S(1)} %get-tuple-element.7.gain_ref), custom_call_target="tpu_custom_call" | custom-call | tf_op jit(solution)/shard_map/transform/pallas_call | solution.py:356
  59.3 30.8 %all_to_all.10 = bf16[128,13,2,128]{3,2,1,0:T(2,128)(2,1)S(1)} all-to-all(bf16[128,13,2,128]{3,2,1,0:T(2,128)(2,1)S(1)} %bitcast.7), channel_id=1, replica_groups=mesh['band'=128,'lev'=2] {'band'}, dimensions={0} | all-to-all | bytes 1703936 | tf_op jit(solution)/shard_map/all_to_all | solution.py:305
  90.1 0.0 copy-done
  90.1 3.1 %unpack.1 = bf16[10,2,4,4,1280]{4,3,2,1,0:T(4,128)(2,1)} custom-call(bf16[3328,128]{1,0:T(8,128)(2,1)S(1)} %bitcast.5, s32[10]{0:T(128)} %points_ref.3, bf16[1280,1280]{1,0:T(8,128)(2,1)S(1)} %copy-done), custom_call_target="tpu_custom_call" | custom-call | tf_op jit(solution)/shard_map/unpack/pallas_call | solution.py:374
Async XLA Ops:
  0.0 48.5 %collective-permute-start = (bf16[5,1281,640]{2,1,0:T(8,128)(2,1)}, bf16[5,1281,640]{2,1,0:T(8,128)(2,1)}, u32[]{:S(2)}, u32[]{:S(2)}) collective-permute-start(bf16[5,1281,640]{2,1,0:T(8,128)(2,1)} %own_ref.1), channel_id=1, source_target_pairs={{0,1},{1,0},{2,3},{3,2},{4,5},{5,4},{6,7},{7,6},{8,9},{9,8},{10,11... | collective-permute-start | bytes 24595208 | tf_op jit(solution)/shard_map/ppermute | solution.py:322
  7.8 40.7 %all-to-all-start = ((bf16[128,13,2,128]{3,2,1,0:T(2,128)(2,1)}), bf16[128,13,2,128]{3,2,1,0:T(2,128)(2,1)S(1)}, u32[]{:S(2)}, u32[]{:S(2)}) async-start(bf16[128,13,2,128]{3,2,1,0:T(2,128)(2,1)} %bitcast.8), calls=%async_computation | async-start | bytes 1703936 | tf_op jit(solution)/shard_map/all_to_all | solution.py:305
  48.5 41.6 %copy-start = (bf16[1280,1280]{1,0:T(8,128)(2,1)S(1)}, bf16[1280,1280]{1,0:T(8,128)(2,1)}, u32[]{:S(2)}) copy-start(bf16[1280,1280]{1,0:T(8,128)(2,1)} %get-tuple-element.8.sel_ref) | copy-start | bytes 9830404

commit v5 on v4

--- a/solution.py
+++ b/solution.py
@@ -18,6 +18,8 @@
 ANY = pl.BlockSpec(memory_space=pl.ANY)
 TILES = 5
 ROWS = 26
+EARLY_SLOTS = (4, 0, 1)
+LATE_SLOTS = (2, 3)
 
 
 def dot(a, b, dims):
@@ -51,16 +53,46 @@
             sel_ref[pl.ds((2 * j + q) * bands, bands), :] = one_hot_rows(listing, j, q, orders, bands)
 
 
-def pack_kernel(x_ref, points_ref, weight_ref, listing_ref, out_ref, x_held, sel_ref, fold, wide, narrow, x_sem, out_sem):
+def pack_kernel(
+    x_ref,
+    points_in,
+    weight_in,
+    order_in,
+    kappa_in,
+    listing_ref,
+    table_ref,
+    out_ref,
+    sel_ref,
+    gain_ref,
+    held_ref,
+    x_held,
+    points_ref,
+    weight_ref,
+    order_ref,
+    kappa_ref,
+    fold,
+    wide,
+    x_sem,
+    own_sem,
+    table_sem,
+):
     rows, _, levels, comps, orders = x_ref.shape
     bands = sel_ref.shape[0] // (2 * TILES)
     vc = levels * comps
     group = 2 * vc
     column = lax.broadcasted_iota(jnp.int32, (comps, orders), 1)
+    scalars = [(points_in, points_ref), (weight_in, weight_ref), (order_in, order_ref), (kappa_in, kappa_ref)]
+    small = [pltpu.make_async_copy(a, b, own_sem.at[n]) for n, (a, b) in enumerate(scalars)]
     loads = [pltpu.make_async_copy(x_ref.at[i], x_held.at[i], x_sem.at[i]) for i in range(rows)]
-    for load in loads:
+    table = [
+        pltpu.make_async_copy(table_ref.at[j], held_ref.at[n], table_sem.at[n]) for n, j in enumerate(EARLY_SLOTS)
+    ]
+    for load in small + loads:
         load.start()
     one_hot(listing_ref, sel_ref)
+    for load in small:
+        load.wait()
+    damping(order_ref, kappa_ref, gain_ref)
     for i in range(rows):
         live = (column <= cutoff_of(points_ref[i], orders)).astype(F32)
         factor = live * weight_ref[i]
@@ -70,6 +102,8 @@
             south = x_held[i, 1, v].astype(F32)
             fold[pl.ds(i * group + v * comps, comps), :] = (north + south) * factor
             fold[pl.ds(i * group + vc + v * comps, comps), :] = (north - south) * factor
+    for load in table:
+        load.start()
     folded = fold[...].astype(BF16)
     per_tile = LANES // group
     for tile in range(3):
@@ -89,26 +123,12 @@
                     one = jnp.concatenate(block(2 * pair + odd), axis=0)
                     message_rows(wide, TILES * pair + 3 * odd + tile, bands)[...] = jnp.transpose(one)
     message_rows(wide, ROWS - 1, bands)[...] = jnp.zeros((bands, LANES), F32)
-    send_out(wide, narrow, out_ref, out_sem)
-
-
-def send_out(wide, narrow, out_ref, sem):
-    parts = sem.shape[0]
-    size = narrow.shape[0] // parts
-    stores = []
-    for n in range(parts):
-        piece = pl.ds(n * size, size)
-        narrow[piece, :] = wide[piece, :].astype(BF16)
-        stores.append(pltpu.make_async_copy(narrow.at[piece], out_ref.at[piece], sem.at[n]))
-        stores[-1].start()
-    for store in stores:
-        store.wait()
-
-
-def between_kernel(order_ref, kappa_ref, listing_ref, gain_ref, sel_out, sel_ref, sel_sem):
-    one_hot(listing_ref, sel_ref)
-    keep = pltpu.make_async_copy(sel_ref, sel_out, sel_sem)
-    keep.start()
+    out_ref[...] = wide[...].astype(BF16)
+    for load in table:
+        load.wait()
+
+
+def damping(order_ref, kappa_ref, gain_ref):
     slots = gain_ref.shape[0]
     orders = gain_ref.shape[2] - LANES
     levels = kappa_ref.shape[1] // 2
@@ -145,13 +165,10 @@
                     leading if q == 0 else jnp.logical_not(leading), odd if p == 1 else jnp.logical_not(odd)
                 )
                 gain_ref[j, pl.ds((2 * q + p) * vc, vc), :] = jnp.where(mask, factor, 0.0)
-    keep.wait()
-
-
-def transform_kernel(
-    got_ref, own_ref, other_ref, gain_ref, out_ref, wide, grid, back, own_held, other_held, own_sem, other_sem
-):
-    slots, nrows, half = own_held.shape
+
+
+def transform_kernel(got_ref, early_ref, table_ref, other_ref, gain_ref, out_ref, late_ref, wide, grid, back, late_sem):
+    slots, nrows, half = other_ref.shape
     orders = nrows - 1
     bands = got_ref.shape[0] // ROWS
     rows = orders // bands
@@ -159,22 +176,15 @@
     lev = lax.axis_index("lev")
     own_first = pl.multiple_of(lev * half, LANES)
     other_first = pl.multiple_of((1 - lev) * half, LANES)
-    middle = orders // 2
-    pieces = [pl.ds(0, middle), pl.ds(middle, nrows - middle)]
-    loads = {}
-    for j in [slots - 1] + list(range(slots - 1)):
-        loads[j] = []
-        for n, piece in enumerate(pieces):
-            own_load = pltpu.make_async_copy(own_ref.at[j, piece], own_held.at[j, piece], own_sem.at[j, n])
-            other_load = pltpu.make_async_copy(other_ref.at[j, piece], other_held.at[j, piece], other_sem.at[j, n])
-            loads[j].append((own_load, other_load))
-
-    def start(j):
-        for both in loads[j]:
-            for load in both:
-                load.start()
-
-    start(4)
+
+    loads = {
+        j: pltpu.make_async_copy(table_ref.at[j], late_ref.at[n], late_sem.at[n]) for n, j in enumerate(LATE_SLOTS)
+    }
+    for load in loads.values():
+        load.start()
+
+    def own_table(j):
+        return early_ref.at[EARLY_SLOTS.index(j)] if j in EARLY_SLOTS else late_ref.at[LATE_SLOTS.index(j)]
 
     def latitude(i, tile):
         return grid.at[pl.ds(tile * orders + i, bands, stride=rows), :]
@@ -195,14 +205,12 @@
 
     def forward(j):
         own, other = columns[j // 2]
-        parts = []
-        for n in range(2):
-            for load in loads[j][n]:
-                load.wait()
-            piece = pl.ds(n * middle, middle)
-            parts.append(dot(own_held[j, piece, :], own, NN) + dot(other_held[j, piece, :], other, NN))
-        coeffs[j] = jnp.concatenate(parts, axis=0)
-        ends[j] = dot(own_held[j, pl.ds(orders, 1), :], own, NN) + dot(other_held[j, pl.ds(orders, 1), :], other, NN)
+        partial = dot(other_ref[j, :orders, :], other, NN)
+        if j in loads:
+            loads[j].wait()
+        table = own_table(j)
+        coeffs[j] = dot(table[:orders, :], own, NN) + partial
+        ends[j] = dot(table[pl.ds(orders, 1), :], own, NN) + dot(other_ref[j, pl.ds(orders, 1), :], other, NN)
 
     def settle(tile):
         inside = [j for j in (2 * tile, 2 * tile + 1) if j < slots]
@@ -216,10 +224,9 @@
             chosen_last[j] = (turned_ends[mine, n : n + 1] * gain_ref[j, :, pl.ds(orders, 1)]).astype(BF16).astype(F32)
 
     def inverse(j):
-        for held, first in ((own_held, own_first), (other_held, other_first)):
-            back[pl.ds(j * four, four), pl.ds(first, half)] = dot(chosen[j], held[j, :orders, :], NN) + chosen_last[
-                j
-            ] * held[j, pl.ds(orders, 1), :].astype(F32)
+        for table, first in ((own_table(j), own_first), (other_ref.at[j], other_first)):
+            last = chosen_last[j] * table[pl.ds(orders, 1), :].astype(F32)
+            back[pl.ds(j * four, four), pl.ds(first, half)] = dot(chosen[j], table[:orders, :], NN) + last
 
     def finish(tile):
         grid[pl.ds(tile * orders, orders), :] = jnp.transpose(back[pl.ds(tile * LANES, LANES), :])
@@ -233,16 +240,12 @@
                 message_rows(wide, TILES * pair + 3 + tile, bands)[...] = odd
 
     arrange(2)
-    start(0)
     arrange(0)
     forward(4)
-    start(1)
     forward(0)
-    start(2)
     settle(2)
     inverse(4)
     forward(1)
-    start(3)
     arrange(1)
     finish(2)
     forward(2)
@@ -318,58 +321,50 @@
     slots, nrows, half = legendre.shape
     group = 2 * levels * comps
     size = (bands * ROWS, LANES)
-    message = pltpu.HBM(size, BF16)
     other = lax.ppermute(legendre, "lev", [(0, 1), (1, 0)])
-    points, weights, listing, kappas = in_hbm(row_points, gauss_weight, pair_order, diffusion.T)
-    packed = pl.pallas_call(
+    points, weights, order, kappas = in_hbm(row_points, gauss_weight, pair_order, diffusion.T)
+    packed, selector, gain, early = pl.pallas_call(
         pack_kernel,
-        out_shape=message,
-        in_specs=[ANY, SMEM, SMEM, VMEM],
-        out_specs=ANY,
+        out_shape=(
+            pltpu.VMEM(size, BF16),
+            pltpu.VMEM((orders, orders), BF16),
+            pltpu.VMEM((slots, 2 * group, orders + LANES), F32),
+            pltpu.VMEM((len(EARLY_SLOTS), nrows, half), BF16),
+        ),
+        in_specs=[ANY, ANY, ANY, ANY, ANY, VMEM, ANY],
+        out_specs=(VMEM,) * 4,
         scratch_shapes=[
             pltpu.VMEM(fourier_in.shape, BF16),
-            pltpu.VMEM((orders, orders), BF16),
+            pltpu.SMEM(row_points.shape, jnp.int32),
+            pltpu.SMEM(gauss_weight.shape, F32),
+            pltpu.SMEM(pair_order.shape, jnp.int32),
+            pltpu.SMEM(diffusion.shape[::-1], F32),
             pltpu.VMEM((group * rows, orders), F32),
             pltpu.VMEM(size, F32),
-            pltpu.VMEM(size, BF16),
             pltpu.SemaphoreType.DMA((rows,)),
             pltpu.SemaphoreType.DMA((4,)),
+            pltpu.SemaphoreType.DMA((len(EARLY_SLOTS),)),
         ],
         compiler_params=kernel_params(16),
         name="pack",
-    )(*in_hbm(fourier_in), points, weights, listing)
+    )(*in_hbm(fourier_in), points, weights, order, kappas, order, *in_hbm(legendre))
     arrived = exchange(packed, bands)
-
-    gain, selector = pl.pallas_call(
-        between_kernel,
-        out_shape=(
-            jax.ShapeDtypeStruct((slots, 2 * group, orders + LANES), F32),
-            pltpu.HBM((orders, orders), BF16),
-        ),
-        in_specs=[SMEM, SMEM, VMEM],
-        out_specs=(VMEM, ANY),
-        scratch_shapes=[pltpu.VMEM((orders, orders), BF16), pltpu.SemaphoreType.DMA(())],
-        compiler_params=kernel_params(16),
-        name="between",
-    )(listing, kappas, listing)
 
     produced = pl.pallas_call(
         transform_kernel,
         out_shape=jax.ShapeDtypeStruct(size, BF16),
-        in_specs=[VMEM, ANY, ANY, VMEM],
+        in_specs=[VMEM, VMEM, ANY, VMEM, VMEM],
         out_specs=VMEM,
         scratch_shapes=[
+            pltpu.VMEM((len(LATE_SLOTS), nrows, half), BF16),
             pltpu.VMEM(size, F32),
             pltpu.VMEM((3 * orders, LANES), F32),
             pltpu.VMEM((3 * LANES, orders), F32),
-            pltpu.VMEM(legendre.shape, BF16),
-            pltpu.VMEM(legendre.shape, BF16),
-            pltpu.SemaphoreType.DMA((slots, 2)),
-            pltpu.SemaphoreType.DMA((slots, 2)),
+            pltpu.SemaphoreType.DMA((len(LATE_SLOTS),)),
         ],
-        compiler_params=kernel_params(40),
+        compiler_params=kernel_params(20),
         name="transform",
-    )(arrived, *in_hbm(legendre, other), gain)
+    )(arrived, *in_vmem(early), *in_hbm(legendre), *in_vmem(other, gain))
     landed = exchange(produced, bands)
     return pl.pallas_call(
         unpack_kernel,

time: 94.2 us -> 92.2 us (0.979)
  blocking collectives: 30.8 us -> 71.3 us
  waiting for transfers between devices: 23 us -> 0.01 us
  starting transfers between devices: 17.2 us -> 3.24 us
  Pallas kernels: 22.2 us -> 16.7 us
    all_to_all x1 -> x2, blocking collectives: 30.8 us -> 71.3 us  [exchange(): lax.all_to_all(shaped, 'band', split_axis=0, concat_axis=0, tiled=True)]
    all_to_all x1 -> x0, waiting for transfers between devices: 23 us -> none  [exchange(): lax.all_to_all(shaped, 'band', split_axis=0, concat_axis=0, tiled=True)]
    all_to_all x1 -> x0, starting transfers between devices: 14 us -> none  [exchange(): lax.all_to_all(shaped, 'band', split_axis=0, concat_axis=0, tiled=True)]
    pallas_call x2 -> x1, Pallas kernels: 8.32 us -> 4.65 us  [on_device(): pl.pallas_call(pack_kernel, out_shape=(pltpu.VMEM(size, BF16), pltpu.VMEM...]
    pallas_call x1, Pallas kernels: 10.8 us -> 8.99 us  [on_device(): pl.pallas_call(transform_kernel, out_shape=jax.ShapeDtypeStruct(size, BF1...]
  transfers between devices with their start and end apart: 2 -> 1, of which waited for: 1 -> 0; matrix products, arithmetic and copies ran while one was open for 0% -> 0% of each run, Pallas kernels for 9% -> 5%
where the time goes in v5:
time: 92.2 us; the launch traced here: 91.4 us
  blocking collectives  71.3 us (77%)
  Pallas kernels  16.7 us (18%)
  starting transfers between devices  3.24 us (4%)
    all_to_all x2, blocking collectives, exchange(): lax.all_to_all(shaped, 'band', split_axis=0, concat_axis=0, tiled=True)  71.3 us
    pallas_call x1, Pallas kernels, on_device(): pl.pallas_call(transform_kernel, out_shape=jax.ShapeDtypeStruct(size, BF1...  8.99 us
    pallas_call x1, Pallas kernels, on_device(): pl.pallas_call(pack_kernel, out_shape=(pltpu.VMEM(size, BF16), pltpu.VMEM...  4.65 us
    ppermute x1, starting transfers between devices, on_device(): other = lax.ppermute(legendre, 'lev', [(0, 1), (1, 0)])  3.24 us
    pallas_call x1, Pallas kernels, on_device(): pl.pallas_call(unpack_kernel, out_shape=jax.ShapeDtypeStruct(fourier_in.s...  3.06 us
  transfers between devices with their start and end apart: 1, of which 0 were waited for; matrix products, arithmetic and copies ran while one was open for 0% of the time, Pallas kernels for 5%

profile of v5, /device:TPU:1, one launch (start us, length us, event | category | flops | bytes accessed | tf_op | source)
XLA Modules:
  0.0 91.4 jit_solution(5026909221068918204)
XLA Ops:
  0.0 3.2 %collective-permute-start = (bf16[5,1281,640]{2,1,0:T(8,128)(2,1)}, bf16[5,1281,640]{2,1,0:T(8,128)(2,1)S(1)}, u32[]{:S(2)}, u32[]{:S(2)}) collective-permute-start(bf16[5,1281,640]{2,1,0:T(8,128)(2,1)} %table_ref.3), channel_id=1, source_target_pairs={{0,1},{1,0},{2,3},{3,2},{4,5},{5,4},{6,7},{7,6},{8,9},{9,8},{10,11... | collective-permute-start | bytes 24595208 | tf_op jit(solution)/shard_map/ppermute | solution.py:324
  3.2 4.7 %pack.1 = (bf16[3328,128]{1,0:T(8,128)(2,1)S(1)}, bf16[1280,1280]{1,0:T(8,128)(2,1)S(1)}, f32[5,64,1408]{2,1,0:T(8,128)S(1)}, bf16[3,1281,640]{2,1,0:T(8,128)(2,1)S(1)}) custom-call(bf16[10,2,4,4,1280]{4,3,2,1,0:T(4,128)(2,1)} %x_ref.1, s32[10]{0:T(128)} %points_ref.1, f32[10]{0:T(128)} %weight_in.1, s32[640]{0:T(1024)} %listing_ref.1, f32[2,8]{1,0:T(2,128)} %bitcast.9, ...), custom_call_target="tpu_custom_call" | custom-call | tf_op jit(solution)/shard_map/pack/pallas_call | solution.py:326
  7.9 40.5 %all_to_all.10 = bf16[128,13,2,128]{3,2,1,0:T(2,128)(2,1)S(1)} all-to-all(bf16[128,13,2,128]{3,2,1,0:T(2,128)(2,1)S(1)} %bitcast.8), channel_id=1, replica_groups=mesh['band'=128,'lev'=2] {'band'}, dimensions={0} | all-to-all | bytes 1703936 | tf_op jit(solution)/shard_map/all_to_all | solution.py:308
  48.4 0.0 collective-permute-done.other_ref
  48.4 9.0 %transform.1 = bf16[3328,128]{1,0:T(8,128)(2,1)S(1)} custom-call(bf16[3328,128]{1,0:T(8,128)(2,1)S(1)} %bitcast.6, bf16[3,1281,640]{2,1,0:T(8,128)(2,1)S(1)} %get-tuple-element.10.early_ref, bf16[5,1281,640]{2,1,0:T(8,128)(2,1)} %table_ref.3, bf16[5,1281,640]{2,1,0:T(8,128)(2,1)S(1)} %collective-permute-done.other_ref, ...), custom_call_target="tpu_custom_call" | custom-call | tf_op jit(solution)/shard_map/transform/pallas_call | solution.py:353
  57.4 30.8 %all_to_all.11 = bf16[128,13,2,128]{3,2,1,0:T(2,128)(2,1)S(1)} all-to-all(bf16[128,13,2,128]{3,2,1,0:T(2,128)(2,1)S(1)} %bitcast.7), channel_id=1, replica_groups=mesh['band'=128,'lev'=2] {'band'}, dimensions={0} | all-to-all | bytes 1703936 | tf_op jit(solution)/shard_map/all_to_all | solution.py:308
  88.2 3.1 %unpack.1 = bf16[10,2,4,4,1280]{4,3,2,1,0:T(4,128)(2,1)} custom-call(bf16[3328,128]{1,0:T(8,128)(2,1)S(1)} %bitcast.5, s32[10]{0:T(128)} %points_ref.1, bf16[1280,1280]{1,0:T(8,128)(2,1)S(1)} %get-tuple-element.12.sel_ref), custom_call_target="tpu_custom_call" | custom-call | tf_op jit(solution)/shard_map/unpack/pallas_call | solution.py:369
Async XLA Ops:
  0.0 48.4 %collective-permute-start = (bf16[5,1281,640]{2,1,0:T(8,128)(2,1)}, bf16[5,1281,640]{2,1,0:T(8,128)(2,1)S(1)}, u32[]{:S(2)}, u32[]{:S(2)}) collective-permute-start(bf16[5,1281,640]{2,1,0:T(8,128)(2,1)} %table_ref.3), channel_id=1, source_target_pairs={{0,1},{1,0},{2,3},{3,2},{4,5},{5,4},{6,7},{7,6},{8,9},{9,8},{10,11... | collective-permute-start | bytes 24595208 | tf_op jit(solution)/shard_map/ppermute | solution.py:324

commit v6 on v5

--- a/solution.py
+++ b/solution.py
@@ -92,6 +92,8 @@
     one_hot(listing_ref, sel_ref)
     for load in small:
         load.wait()
+    for load in table:
+        load.start()
     damping(order_ref, kappa_ref, gain_ref)
     for i in range(rows):
         live = (column <= cutoff_of(points_ref[i], orders)).astype(F32)
@@ -102,8 +104,6 @@
             south = x_held[i, 1, v].astype(F32)
             fold[pl.ds(i * group + v * comps, comps), :] = (north + south) * factor
             fold[pl.ds(i * group + vc + v * comps, comps), :] = (north - south) * factor
-    for load in table:
-        load.start()
     folded = fold[...].astype(BF16)
     per_tile = LANES // group
     for tile in range(3):
@@ -205,11 +205,10 @@
 
     def forward(j):
         own, other = columns[j // 2]
-        partial = dot(other_ref[j, :orders, :], other, NN)
         if j in loads:
             loads[j].wait()
         table = own_table(j)
-        coeffs[j] = dot(table[:orders, :], own, NN) + partial
+        coeffs[j] = dot(table[:orders, :], own, NN) + dot(other_ref[j, :orders, :], other, NN)
         ends[j] = dot(table[pl.ds(orders, 1), :], own, NN) + dot(other_ref[j, pl.ds(orders, 1), :], other, NN)
 
     def settle(tile):
@@ -278,22 +277,20 @@
                 gathered[pl.ds((2 * pair + odd) * group, group), pl.ds(n * bands, bands)] = tiles[n // per_tile][
                     at : at + group
                 ]
-    width = 2 * LANES
+    column = lax.broadcasted_iota(jnp.int32, (comps, orders), 1)
+    cut = rows // 2 * group
     stores = []
-    for n in range(orders // width):
-        block = pl.ds(n * width, width)
-        placed[:, block] = dot(gathered[...], sel_ref[:, block], NN)
-        column = n * width + lax.broadcasted_iota(jnp.int32, (comps, width), 1)
-        for i in range(rows):
-            live = (column <= cutoff_of(points_ref[i], orders)).astype(F32)
-            for v in range(levels):
-                even = placed[pl.ds(i * group + v * comps, comps), block]
-                odd = placed[pl.ds(i * group + vc + v * comps, comps), block]
-                held[i, 0, v, :, block] = ((even + odd) * live).astype(BF16)
-                held[i, 1, v, :, block] = ((even - odd) * live).astype(BF16)
-        stores.append(
-            pltpu.make_async_copy(held.at[:, :, :, :, block], out_ref.at[:, :, :, :, block], out_sem.at[n])
-        )
+    for i in range(rows):
+        if i in (0, rows // 2):
+            lines = pl.ds(i * group, cut)
+            placed[lines, :] = dot(gathered[lines, :], sel_ref[...], NN)
+        live = (column <= cutoff_of(points_ref[i], orders)).astype(F32)
+        for v in range(levels):
+            even = placed[pl.ds(i * group + v * comps, comps), :]
+            odd = placed[pl.ds(i * group + vc + v * comps, comps), :]
+            held[i, 0, v] = ((even + odd) * live).astype(BF16)
+            held[i, 1, v] = ((even - odd) * live).astype(BF16)
+        stores.append(pltpu.make_async_copy(held.at[i], out_ref.at[i], out_sem.at[i]))
         stores[-1].start()
     for store in stores:
         store.wait()
@@ -376,7 +373,7 @@
             pltpu.VMEM((group * rows, orders), BF16),
             pltpu.VMEM((group * rows, orders), F32),
             pltpu.VMEM(fourier_in.shape, BF16),
-            pltpu.SemaphoreType.DMA((orders // (2 * LANES),)),
+            pltpu.SemaphoreType.DMA((rows,)),
         ],
         compiler_params=kernel_params(16),
         name="unpack",

time: 92.2 us -> 91 us (0.987)
  Pallas kernels: 16.7 us -> 15.5 us
where the time goes in v6:
time: 91 us; the launch traced here: 90.3 us
  blocking collectives  71.3 us (78%)
  Pallas kernels  15.5 us (17%)
  starting transfers between devices  3.24 us (4%)
    all_to_all x2, blocking collectives, exchange(): lax.all_to_all(shaped, 'band', split_axis=0, concat_axis=0, tiled=True)  71.3 us
    pallas_call x1, Pallas kernels, on_device(): pl.pallas_call(transform_kernel, out_shape=jax.ShapeDtypeStruct(size, BF1...  8.37 us
    pallas_call x1, Pallas kernels, on_device(): pl.pallas_call(pack_kernel, out_shape=(pltpu.VMEM(size, BF16), pltpu.VMEM...  4.22 us
    ppermute x1, starting transfers between devices, on_device(): other = lax.ppermute(legendre, 'lev', [(0, 1), (1, 0)])  3.24 us
    pallas_call x1, Pallas kernels, on_device(): pl.pallas_call(unpack_kernel, out_shape=jax.ShapeDtypeStruct(fourier_in.s...  2.94 us
  transfers between devices with their start and end apart: 1, of which 0 were waited for; matrix products, arithmetic and copies ran while one was open for 0% of the time, Pallas kernels for 5%

profile of v6, /device:TPU:1, one launch (start us, length us, event | category | flops | bytes accessed | tf_op | source)
XLA Modules:
  0.0 90.3 jit_solution(1783510960636718997)
XLA Ops:
  0.0 3.2 %collective-permute-start = (bf16[5,1281,640]{2,1,0:T(8,128)(2,1)}, bf16[5,1281,640]{2,1,0:T(8,128)(2,1)S(1)}, u32[]{:S(2)}, u32[]{:S(2)}) collective-permute-start(bf16[5,1281,640]{2,1,0:T(8,128)(2,1)} %table_ref.3), channel_id=1, source_target_pairs={{0,1},{1,0},{2,3},{3,2},{4,5},{5,4},{6,7},{7,6},{8,9},{9,8},{10,11... | collective-permute-start | bytes 24595208 | tf_op jit(solution)/shard_map/ppermute | solution.py:321
  3.2 4.2 %pack.1 = (bf16[3328,128]{1,0:T(8,128)(2,1)S(1)}, bf16[1280,1280]{1,0:T(8,128)(2,1)S(1)}, f32[5,64,1408]{2,1,0:T(8,128)S(1)}, bf16[3,1281,640]{2,1,0:T(8,128)(2,1)S(1)}) custom-call(bf16[10,2,4,4,1280]{4,3,2,1,0:T(4,128)(2,1)} %x_ref.1, s32[10]{0:T(128)} %points_ref.1, f32[10]{0:T(128)} %weight_in.1, s32[640]{0:T(1024)} %listing_ref.1, f32[2,8]{1,0:T(2,128)} %bitcast.9, ...), custom_call_target="tpu_custom_call" | custom-call | tf_op jit(solution)/shard_map/pack/pallas_call | solution.py:323
  7.5 40.5 %all_to_all.10 = bf16[128,13,2,128]{3,2,1,0:T(2,128)(2,1)S(1)} all-to-all(bf16[128,13,2,128]{3,2,1,0:T(2,128)(2,1)S(1)} %bitcast.8), channel_id=1, replica_groups=mesh['band'=128,'lev'=2] {'band'}, dimensions={0} | all-to-all | bytes 1703936 | tf_op jit(solution)/shard_map/all_to_all | solution.py:305
  48.0 0.0 collective-permute-done.other_ref
  48.0 8.4 %transform.1 = bf16[3328,128]{1,0:T(8,128)(2,1)S(1)} custom-call(bf16[3328,128]{1,0:T(8,128)(2,1)S(1)} %bitcast.6, bf16[3,1281,640]{2,1,0:T(8,128)(2,1)S(1)} %get-tuple-element.10.early_ref, bf16[5,1281,640]{2,1,0:T(8,128)(2,1)} %table_ref.3, bf16[5,1281,640]{2,1,0:T(8,128)(2,1)S(1)} %collective-permute-done.other_ref, ...), custom_call_target="tpu_custom_call" | custom-call | tf_op jit(solution)/shard_map/transform/pallas_call | solution.py:350
  56.4 30.8 %all_to_all.11 = bf16[128,13,2,128]{3,2,1,0:T(2,128)(2,1)S(1)} all-to-all(bf16[128,13,2,128]{3,2,1,0:T(2,128)(2,1)S(1)} %bitcast.7), channel_id=1, replica_groups=mesh['band'=128,'lev'=2] {'band'}, dimensions={0} | all-to-all | bytes 1703936 | tf_op jit(solution)/shard_map/all_to_all | solution.py:305
  87.2 2.9 %unpack.1 = bf16[10,2,4,4,1280]{4,3,2,1,0:T(4,128)(2,1)} custom-call(bf16[3328,128]{1,0:T(8,128)(2,1)S(1)} %bitcast.5, s32[10]{0:T(128)} %points_ref.1, bf16[1280,1280]{1,0:T(8,128)(2,1)S(1)} %get-tuple-element.12.sel_ref), custom_call_target="tpu_custom_call" | custom-call | tf_op jit(solution)/shard_map/unpack/pallas_call | solution.py:366
Async XLA Ops:
  0.0 48.0 %collective-permute-start = (bf16[5,1281,640]{2,1,0:T(8,128)(2,1)}, bf16[5,1281,640]{2,1,0:T(8,128)(2,1)S(1)}, u32[]{:S(2)}, u32[]{:S(2)}) collective-permute-start(bf16[5,1281,640]{2,1,0:T(8,128)(2,1)} %table_ref.3), channel_id=1, source_target_pairs={{0,1},{1,0},{2,3},{3,2},{4,5},{5,4},{6,7},{7,6},{8,9},{9,8},{10,11... | collective-permute-start | bytes 24595208 | tf_op jit(solution)/shard_map/ppermute | solution.py:321

commit v7 on v6

--- a/solution.py
+++ b/solution.py
@@ -18,8 +18,8 @@
 ANY = pl.BlockSpec(memory_space=pl.ANY)
 TILES = 5
 ROWS = 26
-EARLY_SLOTS = (4, 0, 1)
-LATE_SLOTS = (2, 3)
+EARLY_SLOTS = (4, 0)
+LATE_SLOTS = (1, 2, 3)
 
 
 def dot(a, b, dims):

time: 91 us -> 90.8 us (level)
  transfers between devices with their start and end apart: 1 -> 1, of which waited for: 0 -> 0; matrix products, arithmetic and copies ran while one was open for 0% -> 0% of each run, Pallas kernels for 5% -> 4%
where the time goes in v7:
time: 90.8 us; the launch traced here: 90 us
  blocking collectives  71.3 us (79%)
  Pallas kernels  15.3 us (17%)
  starting transfers between devices  3.24 us (4%)
    all_to_all x2, blocking collectives, exchange(): lax.all_to_all(shaped, 'band', split_axis=0, concat_axis=0, tiled=True)  71.3 us
    pallas_call x1, Pallas kernels, on_device(): pl.pallas_call(transform_kernel, out_shape=jax.ShapeDtypeStruct(size, BF1...  8.55 us
    pallas_call x1, Pallas kernels, on_device(): pl.pallas_call(pack_kernel, out_shape=(pltpu.VMEM(size, BF16), pltpu.VMEM...  3.75 us
    ppermute x1, starting transfers between devices, on_device(): other = lax.ppermute(legendre, 'lev', [(0, 1), (1, 0)])  3.24 us
    pallas_call x1, Pallas kernels, on_device(): pl.pallas_call(unpack_kernel, out_shape=jax.ShapeDtypeStruct(fourier_in.s...  3 us
  transfers between devices with their start and end apart: 1, of which 0 were waited for; matrix products, arithmetic and copies ran while one was open for 0% of the time, Pallas kernels for 4%

profile of v7, /device:TPU:1, one launch (start us, length us, event | category | flops | bytes accessed | tf_op | source)
XLA Modules:
  0.0 90.0 jit_solution(9150412602348763040)
XLA Ops:
  0.0 3.2 %collective-permute-start = (bf16[5,1281,640]{2,1,0:T(8,128)(2,1)}, bf16[5,1281,640]{2,1,0:T(8,128)(2,1)S(1)}, u32[]{:S(2)}, u32[]{:S(2)}) collective-permute-start(bf16[5,1281,640]{2,1,0:T(8,128)(2,1)} %table_ref.3), channel_id=1, source_target_pairs={{0,1},{1,0},{2,3},{3,2},{4,5},{5,4},{6,7},{7,6},{8,9},{9,8},{10,11... | collective-permute-start | bytes 24595208 | tf_op jit(solution)/shard_map/ppermute | solution.py:321
  3.2 3.7 %pack.1 = (bf16[3328,128]{1,0:T(8,128)(2,1)S(1)}, bf16[1280,1280]{1,0:T(8,128)(2,1)S(1)}, f32[5,64,1408]{2,1,0:T(8,128)S(1)}, bf16[2,1281,640]{2,1,0:T(8,128)(2,1)S(1)}) custom-call(bf16[10,2,4,4,1280]{4,3,2,1,0:T(4,128)(2,1)} %x_ref.1, s32[10]{0:T(128)} %points_ref.1, f32[10]{0:T(128)} %weight_in.1, s32[640]{0:T(1024)} %listing_ref.1, f32[2,8]{1,0:T(2,128)} %bitcast.9, ...), custom_call_target="tpu_custom_call" | custom-call | tf_op jit(solution)/shard_map/pack/pallas_call | solution.py:323
  7.0 40.5 %all_to_all.10 = bf16[128,13,2,128]{3,2,1,0:T(2,128)(2,1)S(1)} all-to-all(bf16[128,13,2,128]{3,2,1,0:T(2,128)(2,1)S(1)} %bitcast.8), channel_id=1, replica_groups=mesh['band'=128,'lev'=2] {'band'}, dimensions={0} | all-to-all | bytes 1703936 | tf_op jit(solution)/shard_map/all_to_all | solution.py:305
  47.5 0.0 collective-permute-done.other_ref
  47.5 8.6 %transform.1 = bf16[3328,128]{1,0:T(8,128)(2,1)S(1)} custom-call(bf16[3328,128]{1,0:T(8,128)(2,1)S(1)} %bitcast.6, bf16[2,1281,640]{2,1,0:T(8,128)(2,1)S(1)} %get-tuple-element.10.early_ref, bf16[5,1281,640]{2,1,0:T(8,128)(2,1)} %table_ref.3, bf16[5,1281,640]{2,1,0:T(8,128)(2,1)S(1)} %collective-permute-done.other_ref, ...), custom_call_target="tpu_custom_call" | custom-call | tf_op jit(solution)/shard_map/transform/pallas_call | solution.py:350
  56.1 30.8 %all_to_all.11 = bf16[128,13,2,128]{3,2,1,0:T(2,128)(2,1)S(1)} all-to-all(bf16[128,13,2,128]{3,2,1,0:T(2,128)(2,1)S(1)} %bitcast.7), channel_id=1, replica_groups=mesh['band'=128,'lev'=2] {'band'}, dimensions={0} | all-to-all | bytes 1703936 | tf_op jit(solution)/shard_map/all_to_all | solution.py:305
  86.9 3.0 %unpack.1 = bf16[10,2,4,4,1280]{4,3,2,1,0:T(4,128)(2,1)} custom-call(bf16[3328,128]{1,0:T(8,128)(2,1)S(1)} %bitcast.5, s32[10]{0:T(128)} %points_ref.1, bf16[1280,1280]{1,0:T(8,128)(2,1)S(1)} %get-tuple-element.12.sel_ref), custom_call_target="tpu_custom_call" | custom-call | tf_op jit(solution)/shard_map/unpack/pallas_call | solution.py:366
Async XLA Ops:
  0.0 47.5 %collective-permute-start = (bf16[5,1281,640]{2,1,0:T(8,128)(2,1)}, bf16[5,1281,640]{2,1,0:T(8,128)(2,1)S(1)}, u32[]{:S(2)}, u32[]{:S(2)}) collective-permute-start(bf16[5,1281,640]{2,1,0:T(8,128)(2,1)} %table_ref.3), channel_id=1, source_target_pairs={{0,1},{1,0},{2,3},{3,2},{4,5},{5,4},{6,7},{7,6},{8,9},{9,8},{10,11... | collective-permute-start | bytes 24595208 | tf_op jit(solution)/shard_map/ppermute | solution.py:321

commit v8 on v7

--- a/solution.py
+++ b/solution.py
@@ -59,7 +59,6 @@
     weight_in,
     order_in,
     kappa_in,
-    listing_ref,
     table_ref,
     out_ref,
     sel_ref,
@@ -70,6 +69,7 @@
     weight_ref,
     order_ref,
     kappa_ref,
+    listing_ref,
     fold,
     wide,
     x_sem,
@@ -81,16 +81,23 @@
     vc = levels * comps
     group = 2 * vc
     column = lax.broadcasted_iota(jnp.int32, (comps, orders), 1)
-    scalars = [(points_in, points_ref), (weight_in, weight_ref), (order_in, order_ref), (kappa_in, kappa_ref)]
+    scalars = [
+        (order_in, listing_ref),
+        (order_in, order_ref),
+        (kappa_in, kappa_ref),
+        (points_in, points_ref),
+        (weight_in, weight_ref),
+    ]
     small = [pltpu.make_async_copy(a, b, own_sem.at[n]) for n, (a, b) in enumerate(scalars)]
     loads = [pltpu.make_async_copy(x_ref.at[i], x_held.at[i], x_sem.at[i]) for i in range(rows)]
     table = [
         pltpu.make_async_copy(table_ref.at[j], held_ref.at[n], table_sem.at[n]) for n, j in enumerate(EARLY_SLOTS)
     ]
-    for load in small + loads:
+    for load in small[:1] + loads + small[1:]:
         load.start()
+    small[0].wait()
     one_hot(listing_ref, sel_ref)
-    for load in small:
+    for load in small[1:]:
         load.wait()
     for load in table:
         load.start()
@@ -240,20 +247,20 @@
 
     arrange(2)
     arrange(0)
+    arrange(1)
     forward(4)
     forward(0)
+    forward(1)
+    forward(2)
+    forward(3)
     settle(2)
+    settle(0)
+    settle(1)
     inverse(4)
-    forward(1)
-    arrange(1)
+    inverse(0)
+    inverse(1)
     finish(2)
-    forward(2)
-    settle(0)
-    inverse(0)
-    forward(3)
-    inverse(1)
     finish(0)
-    settle(1)
     inverse(2)
     inverse(3)
     finish(1)
@@ -261,7 +268,9 @@
     out_ref[...] = wide[...].astype(BF16)
 
 
-def unpack_kernel(got_ref, points_ref, sel_ref, out_ref, wide, gathered, placed, held, out_sem):
+def unpack_kernel(got_ref, points_in, sel_ref, out_ref, points_ref, wide, gathered, placed, held, points_sem, out_sem):
+    points_load = pltpu.make_async_copy(points_in, points_ref, points_sem)
+    points_load.start()
     rows, _, levels, comps, orders = out_ref.shape
     bands = got_ref.shape[0] // ROWS
     vc = levels * comps
@@ -280,6 +289,7 @@
     column = lax.broadcasted_iota(jnp.int32, (comps, orders), 1)
     cut = rows // 2 * group
     stores = []
+    points_load.wait()
     for i in range(rows):
         if i in (0, rows // 2):
             lines = pl.ds(i * group, cut)
@@ -328,7 +338,7 @@
             pltpu.VMEM((slots, 2 * group, orders + LANES), F32),
             pltpu.VMEM((len(EARLY_SLOTS), nrows, half), BF16),
         ),
-        in_specs=[ANY, ANY, ANY, ANY, ANY, VMEM, ANY],
+        in_specs=[ANY] * 6,
         out_specs=(VMEM,) * 4,
         scratch_shapes=[
             pltpu.VMEM(fourier_in.shape, BF16),
@@ -336,15 +346,16 @@
             pltpu.SMEM(gauss_weight.shape, F32),
             pltpu.SMEM(pair_order.shape, jnp.int32),
             pltpu.SMEM(diffusion.shape[::-1], F32),
+            pltpu.VMEM(pair_order.shape, jnp.int32),
             pltpu.VMEM((group * rows, orders), F32),
             pltpu.VMEM(size, F32),
             pltpu.SemaphoreType.DMA((rows,)),
-            pltpu.SemaphoreType.DMA((4,)),
+            pltpu.SemaphoreType.DMA((5,)),
             pltpu.SemaphoreType.DMA((len(EARLY_SLOTS),)),
         ],
         compiler_params=kernel_params(16),
         name="pack",
-    )(*in_hbm(fourier_in), points, weights, order, kappas, order, *in_hbm(legendre))
+    )(*in_hbm(fourier_in), points, weights, order, kappas, *in_hbm(legendre))
     arrived = exchange(packed, bands)
 
     produced = pl.pallas_call(
@@ -366,13 +377,15 @@
     return pl.pallas_call(
         unpack_kernel,
         out_shape=jax.ShapeDtypeStruct(fourier_in.shape, BF16),
-        in_specs=[VMEM, SMEM, VMEM],
+        in_specs=[VMEM, ANY, VMEM],
         out_specs=ANY,
         scratch_shapes=[
+            pltpu.SMEM(row_points.shape, jnp.int32),
             pltpu.VMEM(size, F32),
             pltpu.VMEM((group * rows, orders), BF16),
             pltpu.VMEM((group * rows, orders), F32),
             pltpu.VMEM(fourier_in.shape, BF16),
+            pltpu.SemaphoreType.DMA(()),
             pltpu.SemaphoreType.DMA((rows,)),
         ],
         compiler_params=kernel_params(16),

time: 90.8 us -> 90.8 us (level)
  no operation moved by 1% of the time
where the time goes in v8:
time: 90.8 us; the launch traced here: 90.1 us
  blocking collectives  71.3 us (79%)
  Pallas kernels  15.3 us (17%)
  starting transfers between devices  3.24 us (4%)
    all_to_all x2, blocking collectives, exchange(): lax.all_to_all(shaped, 'band', split_axis=0, concat_axis=0, tiled=True)  71.3 us
    pallas_call x1, Pallas kernels, on_device(): pl.pallas_call(transform_kernel, out_shape=jax.ShapeDtypeStruct(size, BF1...  8.43 us
    pallas_call x1, Pallas kernels, on_device(): pl.pallas_call(pack_kernel, out_shape=(pltpu.VMEM(size, BF16), pltpu.VMEM...  3.91 us
    ppermute x1, starting transfers between devices, on_device(): other = lax.ppermute(legendre, 'lev', [(0, 1), (1, 0)])  3.24 us
    pallas_call x1, Pallas kernels, on_device(): pl.pallas_call(unpack_kernel, out_shape=jax.ShapeDtypeStruct(fourier_in.s...  3.01 us
  transfers between devices with their start and end apart: 1, of which 0 were waited for; matrix products, arithmetic and copies ran while one was open for 0% of the time, Pallas kernels for 4%

profile of v8, /device:TPU:1, one launch (start us, length us, event | category | flops | bytes accessed | tf_op | source)
XLA Modules:
  0.0 90.1 jit_solution(12894536438596523149)
XLA Ops:
  0.0 3.2 %collective-permute-start = (bf16[5,1281,640]{2,1,0:T(8,128)(2,1)}, bf16[5,1281,640]{2,1,0:T(8,128)(2,1)S(1)}, u32[]{:S(2)}, u32[]{:S(2)}) collective-permute-start(bf16[5,1281,640]{2,1,0:T(8,128)(2,1)} %table_ref.3), channel_id=1, source_target_pairs={{0,1},{1,0},{2,3},{3,2},{4,5},{5,4},{6,7},{7,6},{8,9},{9,8},{10,11... | collective-permute-start | bytes 24595208 | tf_op jit(solution)/shard_map/ppermute | solution.py:331
  3.2 3.9 %pack.1 = (bf16[3328,128]{1,0:T(8,128)(2,1)S(1)}, bf16[1280,1280]{1,0:T(8,128)(2,1)S(1)}, f32[5,64,1408]{2,1,0:T(8,128)S(1)}, bf16[2,1281,640]{2,1,0:T(8,128)(2,1)S(1)}) custom-call(bf16[10,2,4,4,1280]{4,3,2,1,0:T(4,128)(2,1)} %x_ref.1, s32[10]{0:T(128)} %points_in.3, f32[10]{0:T(128)} %weight_in.1, s32[640]{0:T(1024)} %order_in.1, f32[2,8]{1,0:T(2,128)} %bitcast.9, ...), custom_call_target="tpu_custom_call" | custom-call | tf_op jit(solution)/shard_map/pack/pallas_call | solution.py:333
  7.2 40.5 %all_to_all.10 = bf16[128,13,2,128]{3,2,1,0:T(2,128)(2,1)S(1)} all-to-all(bf16[128,13,2,128]{3,2,1,0:T(2,128)(2,1)S(1)} %bitcast.8), channel_id=1, replica_groups=mesh['band'=128,'lev'=2] {'band'}, dimensions={0} | all-to-all | bytes 1703936 | tf_op jit(solution)/shard_map/all_to_all | solution.py:315
  47.7 0.0 collective-permute-done.other_ref
  47.7 8.4 %transform.1 = bf16[3328,128]{1,0:T(8,128)(2,1)S(1)} custom-call(bf16[3328,128]{1,0:T(8,128)(2,1)S(1)} %bitcast.6, bf16[2,1281,640]{2,1,0:T(8,128)(2,1)S(1)} %get-tuple-element.10.early_ref, bf16[5,1281,640]{2,1,0:T(8,128)(2,1)} %table_ref.3, bf16[5,1281,640]{2,1,0:T(8,128)(2,1)S(1)} %collective-permute-done.other_ref, ...), custom_call_target="tpu_custom_call" | custom-call | tf_op jit(solution)/shard_map/transform/pallas_call | solution.py:361
  56.1 30.8 %all_to_all.11 = bf16[128,13,2,128]{3,2,1,0:T(2,128)(2,1)S(1)} all-to-all(bf16[128,13,2,128]{3,2,1,0:T(2,128)(2,1)S(1)} %bitcast.7), channel_id=1, replica_groups=mesh['band'=128,'lev'=2] {'band'}, dimensions={0} | all-to-all | bytes 1703936 | tf_op jit(solution)/shard_map/all_to_all | solution.py:315
  86.9 3.0 %unpack.1 = bf16[10,2,4,4,1280]{4,3,2,1,0:T(4,128)(2,1)} custom-call(bf16[3328,128]{1,0:T(8,128)(2,1)S(1)} %bitcast.5, s32[10]{0:T(128)} %points_in.3, bf16[1280,1280]{1,0:T(8,128)(2,1)S(1)} %get-tuple-element.12.sel_ref), custom_call_target="tpu_custom_call" | custom-call | tf_op jit(solution)/shard_map/unpack/pallas_call | solution.py:377
Async XLA Ops:
  0.0 47.7 %collective-permute-start = (bf16[5,1281,640]{2,1,0:T(8,128)(2,1)}, bf16[5,1281,640]{2,1,0:T(8,128)(2,1)S(1)}, u32[]{:S(2)}, u32[]{:S(2)}) collective-permute-start(bf16[5,1281,640]{2,1,0:T(8,128)(2,1)} %table_ref.3), channel_id=1, source_target_pairs={{0,1},{1,0},{2,3},{3,2},{4,5},{5,4},{6,7},{7,6},{8,9},{9,8},{10,11... | collective-permute-start | bytes 24595208 | tf_op jit(solution)/shard_map/ppermute | solution.py:331
